TPU v7x, 32 devices: a whole 2x2x4 slice. The times are simulated.
32 devices in a mesh: rows: 4 (over x, core), seq: 8 (over z, y).
Axes of the slice: x: 2, y: 2, z: 4, core: 2. Of those that a mesh axis runs over, the one named last changes fastest.
Arguments:
- noisy_mel: bfloat16 [4, 2048, 100], P('rows', 'seq'), may hold values from -6 to 6
- cond_mel: bfloat16 [4, 2048, 100], P('rows', 'seq'), may hold values from -6 to 6
- text_feats: bfloat16 [4, 2048, 512], P('rows', 'seq'), may hold values from -6 to 6
- segment_ids: int32 [4, 2048], P('rows', 'seq'), may hold values from 0 to 3, as said below
- drop_cond: int32 [4, 4], P('rows'), may hold values 0 or 1
- drop_text: int32 [4, 4], P('rows'), may hold values 0 or 1
- time_index: int32 [4, 4], P('rows'), may hold values from 0 to 31
- time_table: float32 [32, 1024], replicated, may hold values from -4 to 4
- w_input: bfloat16 [712, 1024], replicated, may hold values from -0.21875 to 0.21875
- b_input: float32 [1024], replicated, may hold values from -3 to 3
- w_ada: bfloat16 [1024, 6144], replicated, may hold values from -0.1875 to 0.1875
- b_ada: float32 [6144], replicated, may hold values from -3 to 3
- w_query: bfloat16 [1024, 1024], replicated, may hold values from -0.1875 to 0.1875
- b_query: float32 [1024], replicated, may hold values from -3 to 3
- w_key: bfloat16 [1024, 1024], replicated, may hold values from -0.1875 to 0.1875
- b_key: float32 [1024], replicated, may hold values from -3 to 3
- w_value: bfloat16 [1024, 1024], replicated, may hold values from -0.1875 to 0.1875
- b_value: float32 [1024], replicated, may hold values from -3 to 3
- w_out: bfloat16 [1024, 1024], replicated, may hold values from -3 to 3
- b_out: float32 [1024], replicated, may hold values from -7.5 to 7.5
- w_up: bfloat16 [1024, 2048], replicated, may hold values from -0.1875 to 0.1875
- b_up: float32 [2048], replicated, may hold values from -3 to 3
- w_down: bfloat16 [2048, 1024], replicated, may hold values from -0.125 to 0.125
- b_down: float32 [1024], replicated, may hold values from -7.5 to 7.5
- cotangent: bfloat16 [4, 2048, 1024], P('rows', 'seq'), may hold values from -6 to 6
Outputs:
- layer_out: bfloat16 [4, 2048, 1024], P('rows', 'seq')
- grad_noisy: float32 [4, 2048, 100], P('rows', 'seq')
- grad_cond: float32 [4, 2048, 100], P('rows', 'seq')
- grad_text: float32 [4, 2048, 512], P('rows', 'seq')
- grad_table: float32 [32, 1024], P(None, ('rows', 'seq'))
- grad_w_input: float32 [712, 1024], P(None, ('rows', 'seq'))
- grad_b_input: float32 [1024], P(('rows', 'seq'))
- grad_w_ada: float32 [1024, 6144], P(('rows', 'seq'))
- grad_b_ada: float32 [6144], P(('rows', 'seq'))
- grad_w_query: float32 [1024, 1024], P(('rows', 'seq'))
- grad_b_query: float32 [1024], P(('rows', 'seq'))
- grad_w_key: float32 [1024, 1024], P(('rows', 'seq'))
- grad_b_key: float32 [1024], P(('rows', 'seq'))
- grad_w_value: float32 [1024, 1024], P(('rows', 'seq'))
- grad_b_value: float32 [1024], P(('rows', 'seq'))
- grad_w_out: float32 [1024, 1024], P(('rows', 'seq'))
- grad_b_out: float32 [1024], P(('rows', 'seq'))
- grad_w_up: float32 [1024, 2048], P(('rows', 'seq'))
- grad_b_up: float32 [2048], P(('rows', 'seq'))
- grad_w_down: float32 [2048, 1024], P(('rows', 'seq'))
- grad_b_down: float32 [1024], P(('rows', 'seq'))
Inputs may be any that keep to these rules, and one draw needn't show every extreme that they name: `segment_ids`: along each row the ids never fall, and every id from 0 to 3 occurs.
All inputs are finite; a program needn't handle non-finite values. No bound on the sum of `drop_cond` or of `drop_text` on one device may be relied on, other than what follows from the above.
Results may differ from a plain program's by a relative error of at most 0.0213.
Values may be sent and summed in bfloat16 or wider, within the bound.
A program may use at most 256 MiB of HBM per device.

v0:
```python
import math

import jax
import jax.numpy as jnp
from jax import lax
from jax.sharding import PartitionSpec as P

HEADS = 16


precise = lax.Precision.HIGHEST


def layer_norm(values):
    centred = values - jnp.mean(values, axis=-1, keepdims=True)
    return centred * lax.rsqrt(jnp.mean(centred * centred, axis=-1, keepdims=True) + 1e-06)


def gelu_tanh(values):
    return jax.nn.gelu(values, approximate=True)


def rotary(values, positions, head_count, direction):
    row_count, model_width = values.shape
    head_width = model_width // head_count
    inverse_freq = jnp.power(
        10000.0, -jnp.arange(0, head_width, 2).astype(jnp.float32) / head_width
    )
    angles = positions[:, None] * inverse_freq[None, :]
    cosine = jnp.cos(angles)[:, None, :]
    sine = direction * jnp.sin(angles)[:, None, :]
    paired = values.reshape(row_count, head_count, head_width // 2, 2)
    first = paired[..., 0]
    second = paired[..., 1]
    turned = jnp.stack([first * cosine - second * sine, second * cosine + first * sine], axis=-1)
    return turned.reshape(row_count, model_width)


def over_blocks(block_fn, running, arrays):
    row_count = arrays[0].shape[0]
    block_rows = math.gcd(row_count, 512)
    shaped = tuple(
        (array.reshape((row_count // block_rows, block_rows) + array.shape[1:]) for array in arrays)
    )
    offsets = jnp.arange(row_count // block_rows, dtype=jnp.int32) * block_rows

    def advance(carried, element):
        return (block_fn(carried, element[0], element[1]), None)

    running, unused = lax.scan(advance, running, (shaped, offsets))
    return running


def three_parts(values):
    leading = values.astype(jnp.bfloat16)
    remainder = values - leading.astype(jnp.float32)
    second = remainder.astype(jnp.bfloat16)
    third = (remainder - second.astype(jnp.float32)).astype(jnp.bfloat16)
    return (leading, second, third)


def shards(
    noisy_mel,
    cond_mel,
    text_feats,
    segment_ids,
    drop_cond,
    drop_text,
    time_index,
    time_table,
    w_input,
    b_input,
    w_ada,
    b_ada,
    w_query,
    b_query,
    w_key,
    b_key,
    w_value,
    b_value,
    w_out,
    b_out,
    w_up,
    b_up,
    w_down,
    b_down,
    cotangent,
):
    frames = noisy_mel.shape[1]
    model_width = w_query.shape[0]
    head_count = HEADS
    head_width = model_width // head_count
    score_scale = 1.0 / math.sqrt(head_width)
    mel_width = noisy_mel.shape[2]
    table_rows = time_table.shape[0]
    segments = drop_cond.shape[1]
    local_seg = segment_ids[0]
    row_seg = lax.all_gather(local_seg, "seq", axis=0, tiled=True)
    member = local_seg[:, None] == jnp.arange(segments, dtype=jnp.int32)[None, :]
    keep_cond = 1 - jnp.sum(jnp.where(member, drop_cond[0][None, :], 0), axis=1)
    keep_text = 1 - jnp.sum(jnp.where(member, drop_text[0][None, :], 0), axis=1)
    time_row = jnp.sum(jnp.where(member, time_index[0][None, :], 0), axis=1)
    time_onehot = (time_row[:, None] == jnp.arange(table_rows, dtype=jnp.int32)[None, :]).astype(
        jnp.float32
    )
    features = jnp.concatenate(
        [
            noisy_mel[0],
            cond_mel[0] * keep_cond[:, None].astype(jnp.bfloat16),
            text_feats[0] * keep_text[:, None].astype(jnp.bfloat16),
        ],
        axis=1,
    )
    stream = jnp.dot(features, w_input, preferred_element_type=jnp.float32) + b_input
    silu_table_full, silu_back = jax.vjp(jax.nn.silu, time_table)
    silu_slope = silu_back(jnp.ones_like(time_table))[0]
    silu_table = silu_table_full.astype(jnp.bfloat16)
    mod_table = jnp.dot(silu_table, w_ada, preferred_element_type=jnp.float32) + b_ada
    modulation = jnp.dot(time_onehot, mod_table, precision=precise)
    shift_attn, scale_attn, gate_attn, shift_ffn, scale_ffn, gate_ffn = jnp.split(
        modulation, 6, axis=1
    )
    norm_attn, back_attn = jax.vjp(layer_norm, stream)
    attn_in = (norm_attn * (1.0 + scale_attn) + shift_attn).astype(jnp.bfloat16)
    positions = (lax.axis_index("seq") * frames + jnp.arange(frames, dtype=jnp.int32)).astype(
        jnp.float32
    )
    query_raw = jnp.dot(attn_in, w_query, preferred_element_type=jnp.float32) + b_query
    key_raw = jnp.dot(attn_in, w_key, preferred_element_type=jnp.float32) + b_key
    value_raw = jnp.dot(attn_in, w_value, preferred_element_type=jnp.float32) + b_value
    query_rot = rotary(query_raw, positions, head_count, 1.0).astype(jnp.bfloat16)
    key_rot = rotary(key_raw, positions, head_count, 1.0).astype(jnp.bfloat16)
    value_low = value_raw.astype(jnp.bfloat16)
    query_heads = query_rot.reshape(frames, head_count, head_width)
    key_heads = key_rot.reshape(frames, head_count, head_width)
    value_heads = value_low.reshape(frames, head_count, head_width)

    def key_block(running, pieces, first_row):
        running_max, row_total, weighted = running
        key_rows, value_rows = pieces
        rows_here = key_rows.shape[0]
        key_seg = lax.dynamic_slice_in_dim(row_seg, first_row, rows_here)
        allowed = (local_seg[:, None] == key_seg[None, :])[None]
        scores = (
            jnp.einsum(
                "qhd,khd->hqk",
                query_heads,
                key_rows.reshape(rows_here, head_count, head_width),
                preferred_element_type=jnp.float32,
            )
            * score_scale
        )
        scores = jnp.where(allowed, scores, -1e30)
        new_max = jnp.maximum(running_max, jnp.max(scores, axis=-1))
        weights = jnp.where(allowed, jnp.exp(scores - new_max[..., None]), 0.0)
        factor = jnp.exp(running_max - new_max)
        row_total = row_total * factor + jnp.sum(weights, axis=-1)
        weighted = weighted * factor.T[:, :, None] + jnp.einsum(
            "hqk,khd->qhd",
            weights.astype(jnp.bfloat16),
            value_rows.reshape(rows_here, head_count, head_width),
            preferred_element_type=jnp.float32,
        )
        return (new_max, row_total, weighted)

    empty_heads = jnp.zeros((frames, head_count, head_width), jnp.float32)
    start_state = (
        jnp.full((head_count, frames), -1e30, jnp.float32),
        jnp.zeros((head_count, frames), jnp.float32),
        empty_heads,
    )
    running_max, row_total, weighted = over_blocks(
        key_block,
        start_state,
        (
            lax.all_gather(key_rot, "seq", axis=0, tiled=True),
            lax.all_gather(value_low, "seq", axis=0, tiled=True),
        ),
    )
    attended = weighted / row_total.T[:, :, None]
    log_total = running_max + jnp.log(row_total)
    attended_low = attended.reshape(frames, model_width).astype(jnp.bfloat16)
    attn_branch = jnp.dot(attended_low, w_out, preferred_element_type=jnp.float32) + b_out
    middle = stream + gate_attn * attn_branch
    norm_ffn, back_ffn = jax.vjp(layer_norm, middle)
    ffn_in = (norm_ffn * (1.0 + scale_ffn) + shift_ffn).astype(jnp.bfloat16)
    up_value = jnp.dot(ffn_in, w_up, preferred_element_type=jnp.float32) + b_up
    activated, gelu_back = jax.vjp(gelu_tanh, up_value)
    activated_low = activated.astype(jnp.bfloat16)
    ffn_branch = jnp.dot(activated_low, w_down, preferred_element_type=jnp.float32) + b_down
    layer_out = (middle + gate_ffn * ffn_branch).astype(jnp.bfloat16)
    grad_output = cotangent[0].astype(jnp.float32)
    grad_ffn = (grad_output * gate_ffn).astype(jnp.bfloat16)
    grad_gate_ffn = grad_output * ffn_branch
    part_w_down = jnp.dot(activated_low.T, grad_ffn, preferred_element_type=jnp.float32)
    part_b_down = jnp.sum(grad_ffn.astype(jnp.float32), axis=0)
    grad_up = gelu_back(jnp.dot(grad_ffn, w_down.T, preferred_element_type=jnp.float32))[0].astype(
        jnp.bfloat16
    )
    part_w_up = jnp.dot(ffn_in.T, grad_up, preferred_element_type=jnp.float32)
    part_b_up = jnp.sum(grad_up.astype(jnp.float32), axis=0)
    grad_ffn_in = jnp.dot(grad_up, w_up.T, preferred_element_type=jnp.float32)
    grad_scale_ffn = grad_ffn_in * norm_ffn
    grad_middle = grad_output + back_ffn(grad_ffn_in * (1.0 + scale_ffn))[0]
    grad_attn = (grad_middle * gate_attn).astype(jnp.bfloat16)
    grad_gate_attn = grad_middle * attn_branch
    part_w_out = jnp.dot(attended_low.T, grad_attn, preferred_element_type=jnp.float32)
    part_b_out = jnp.sum(grad_attn.astype(jnp.float32), axis=0)
    grad_attended = jnp.dot(grad_attn, w_out.T, preferred_element_type=jnp.float32).astype(
        jnp.bfloat16
    )
    grad_heads = grad_attended.reshape(frames, head_count, head_width)
    row_delta = jnp.sum(grad_heads.astype(jnp.float32) * attended, axis=-1).T
    total_rows, delta_rows = (
        lax.all_gather(log_total, "seq", axis=1, tiled=True),
        lax.all_gather(row_delta, "seq", axis=1, tiled=True),
    )

    def query_grad_block(running, pieces, first_row):
        key_rows, value_rows = pieces
        rows_here = key_rows.shape[0]
        key_seg = lax.dynamic_slice_in_dim(row_seg, first_row, rows_here)
        allowed = (local_seg[:, None] == key_seg[None, :])[None]
        key_part = key_rows.reshape(rows_here, head_count, head_width)
        scores = (
            jnp.einsum("qhd,khd->hqk", query_heads, key_part, preferred_element_type=jnp.float32)
            * score_scale
        )
        probability = jnp.where(allowed, jnp.exp(scores - log_total[..., None]), 0.0)
        grad_probs = jnp.einsum(
            "qhd,khd->hqk",
            grad_heads,
            value_rows.reshape(rows_here, head_count, head_width),
            preferred_element_type=jnp.float32,
        )
        grad_scores = (probability * (grad_probs - row_delta[..., None])).astype(jnp.bfloat16)
        return (
            running
            + jnp.einsum("hqk,khd->qhd", grad_scores, key_part, preferred_element_type=jnp.float32)
            * score_scale
        )

    grad_query_heads = over_blocks(
        query_grad_block,
        empty_heads,
        (
            lax.all_gather(key_rot, "seq", axis=0, tiled=True),
            lax.all_gather(value_low, "seq", axis=0, tiled=True),
        ),
    )

    def key_grad_block(running, pieces, first_row):
        grad_key_acc, grad_value_acc = running
        query_rows, grad_rows = pieces
        rows_here = query_rows.shape[0]
        query_seg = lax.dynamic_slice_in_dim(row_seg, first_row, rows_here)
        allowed = (query_seg[:, None] == local_seg[None, :])[None]
        total_part = lax.dynamic_slice_in_dim(total_rows, first_row, rows_here, 1)
        delta_part = lax.dynamic_slice_in_dim(delta_rows, first_row, rows_here, 1)
        query_part = query_rows.reshape(rows_here, head_count, head_width)
        grad_part = grad_rows.reshape(rows_here, head_count, head_width)
        scores = (
            jnp.einsum("qhd,khd->hqk", query_part, key_heads, preferred_element_type=jnp.float32)
            * score_scale
        )
        probability = jnp.where(allowed, jnp.exp(scores - total_part[..., None]), 0.0)
        grad_value_acc = grad_value_acc + jnp.einsum(
            "hqk,qhd->khd",
            probability.astype(jnp.bfloat16),
            grad_part,
            preferred_element_type=jnp.float32,
        )
        grad_probs = jnp.einsum(
            "qhd,khd->hqk", grad_part, value_heads, preferred_element_type=jnp.float32
        )
        grad_scores = (probability * (grad_probs - delta_part[..., None])).astype(jnp.bfloat16)
        grad_key_acc = (
            grad_key_acc
            + jnp.einsum(
                "hqk,qhd->khd", grad_scores, query_part, preferred_element_type=jnp.float32
            )
            * score_scale
        )
        return (grad_key_acc, grad_value_acc)

    grad_key_heads, grad_value_heads = over_blocks(
        key_grad_block,
        (empty_heads, empty_heads),
        (
            lax.all_gather(query_rot, "seq", axis=0, tiled=True),
            lax.all_gather(grad_attended, "seq", axis=0, tiled=True),
        ),
    )
    grad_query = rotary(
        grad_query_heads.reshape(frames, model_width), positions, head_count, -1.0
    ).astype(jnp.bfloat16)
    grad_key = rotary(
        grad_key_heads.reshape(frames, model_width), positions, head_count, -1.0
    ).astype(jnp.bfloat16)
    grad_value = grad_value_heads.reshape(frames, model_width).astype(jnp.bfloat16)
    part_w_query = jnp.dot(attn_in.T, grad_query, preferred_element_type=jnp.float32)
    part_b_query = jnp.sum(grad_query.astype(jnp.float32), axis=0)
    part_w_key = jnp.dot(attn_in.T, grad_key, preferred_element_type=jnp.float32)
    part_b_key = jnp.sum(grad_key.astype(jnp.float32), axis=0)
    part_w_value = jnp.dot(attn_in.T, grad_value, preferred_element_type=jnp.float32)
    part_b_value = jnp.sum(grad_value.astype(jnp.float32), axis=0)
    grad_attn_in = (
        jnp.dot(grad_query, w_query.T, preferred_element_type=jnp.float32)
        + jnp.dot(grad_key, w_key.T, preferred_element_type=jnp.float32)
        + jnp.dot(grad_value, w_value.T, preferred_element_type=jnp.float32)
    )
    grad_scale_attn = grad_attn_in * norm_attn
    grad_stream = (grad_middle + back_attn(grad_attn_in * (1.0 + scale_attn))[0]).astype(
        jnp.bfloat16
    )
    part_w_input = jnp.dot(features.T, grad_stream, preferred_element_type=jnp.float32)
    part_b_input = jnp.sum(grad_stream.astype(jnp.float32), axis=0)
    grad_features = jnp.dot(grad_stream, w_input.T, preferred_element_type=jnp.float32)
    grad_noisy = grad_features[:, :mel_width]
    grad_cond = grad_features[:, mel_width : 2 * mel_width] * keep_cond[:, None].astype(jnp.float32)
    grad_text = grad_features[:, 2 * mel_width :] * keep_text[:, None].astype(jnp.float32)
    grad_modulation = jnp.concatenate(
        [grad_attn_in, grad_scale_attn, grad_gate_attn, grad_ffn_in, grad_scale_ffn, grad_gate_ffn],
        axis=1,
    )
    grad_mod_table = jnp.dot(time_onehot.T, grad_modulation, precision=precise)
    local_parts = three_parts(grad_mod_table)
    part_w_ada = sum(
        (jnp.dot(silu_table.T, piece, preferred_element_type=jnp.float32) for piece in local_parts)
    )
    part_b_ada = jnp.sum(grad_mod_table, axis=0)
    part_table = (
        sum((jnp.dot(piece, w_ada.T, preferred_element_type=jnp.float32) for piece in local_parts))
        * silu_slope
    )
    (
        grad_w_input,
        grad_b_input,
        grad_w_ada,
        grad_b_ada,
        grad_w_query,
        grad_b_query,
        grad_w_key,
        grad_b_key,
        grad_w_value,
        grad_b_value,
        grad_w_out,
        grad_b_out,
        grad_w_up,
        grad_b_up,
        grad_w_down,
        grad_b_down,
        grad_table,
    ) = (
        lax.psum_scatter(part_w_input, ("rows", "seq"), scatter_dimension=1, tiled=True),
        lax.psum_scatter(part_b_input, ("rows", "seq"), scatter_dimension=0, tiled=True),
        lax.psum_scatter(part_w_ada, ("rows", "seq"), scatter_dimension=0, tiled=True),
        lax.psum_scatter(part_b_ada, ("rows", "seq"), scatter_dimension=0, tiled=True),
        lax.psum_scatter(part_w_query, ("rows", "seq"), scatter_dimension=0, tiled=True),
        lax.psum_scatter(part_b_query, ("rows", "seq"), scatter_dimension=0, tiled=True),
        lax.psum_scatter(part_w_key, ("rows", "seq"), scatter_dimension=0, tiled=True),
        lax.psum_scatter(part_b_key, ("rows", "seq"), scatter_dimension=0, tiled=True),
        lax.psum_scatter(part_w_value, ("rows", "seq"), scatter_dimension=0, tiled=True),
        lax.psum_scatter(part_b_value, ("rows", "seq"), scatter_dimension=0, tiled=True),
        lax.psum_scatter(part_w_out, ("rows", "seq"), scatter_dimension=0, tiled=True),
        lax.psum_scatter(part_b_out, ("rows", "seq"), scatter_dimension=0, tiled=True),
        lax.psum_scatter(part_w_up, ("rows", "seq"), scatter_dimension=0, tiled=True),
        lax.psum_scatter(part_b_up, ("rows", "seq"), scatter_dimension=0, tiled=True),
        lax.psum_scatter(part_w_down, ("rows", "seq"), scatter_dimension=0, tiled=True),
        lax.psum_scatter(part_b_down, ("rows", "seq"), scatter_dimension=0, tiled=True),
        lax.psum_scatter(part_table, ("rows", "seq"), scatter_dimension=1, tiled=True),
    )
    return (
        layer_out[None],
        grad_noisy[None],
        grad_cond[None],
        grad_text[None],
        grad_table,
        grad_w_input,
        grad_b_input,
        grad_w_ada,
        grad_b_ada,
        grad_w_query,
        grad_b_query,
        grad_w_key,
        grad_b_key,
        grad_w_value,
        grad_b_value,
        grad_w_out,
        grad_b_out,
        grad_w_up,
        grad_b_up,
        grad_w_down,
        grad_b_down,
    )


def solution(mesh):
    in_specs = (
        P("rows", "seq", None),
        P("rows", "seq", None),
        P("rows", "seq", None),
        P("rows", "seq"),
        P("rows", None),
        P("rows", None),
        P("rows", None),
        P(),
        P(),
        P(),
        P(),
        P(),
        P(),
        P(),
        P(),
        P(),
        P(),
        P(),
        P(),
        P(),
        P(),
        P(),
        P(),
        P(),
        P("rows", "seq", None),
    )
    out_specs = (
        P("rows", "seq", None),
        P("rows", "seq", None),
        P("rows", "seq", None),
        P("rows", "seq", None),
        P(None, ("rows", "seq")),
        P(None, ("rows", "seq")),
        P(("rows", "seq")),
        P(("rows", "seq"), None),
        P(("rows", "seq")),
        P(("rows", "seq"), None),
        P(("rows", "seq")),
        P(("rows", "seq"), None),
        P(("rows", "seq")),
        P(("rows", "seq"), None),
        P(("rows", "seq")),
        P(("rows", "seq"), None),
        P(("rows", "seq")),
        P(("rows", "seq"), None),
        P(("rows", "seq")),
        P(("rows", "seq"), None),
        P(("rows", "seq")),
    )
    return jax.shard_map(shards, mesh=mesh, in_specs=in_specs, out_specs=out_specs, check_vma=False)
```

profile of v0, /device:TPU:0, one launch (start us, length us, event | category | flops | bytes accessed | tf_op | source)
XLA Modules:
  0.0 2040.5 jit_solution(7536589635085835985)
XLA Ops:
  16.0 6.8 convolution_add_fusion
  65.7 22.9 %all-gather = s32[1,2048]{1,0:T(1,128)S(1)} all-gather(s32[1,256]{1,0:T(1,128)S(1)} %copy-done.42), channel_id=2, replica_groups=mesh['rows'=4,'seq'=8] {'seq'}, dimensions={1}, use_global_device_ids=true | all-gather | bytes 9216 | tf_op jit(solution)/shard_map/all_gather | solution.py:98
  95.1 12.2 all-gather.8.cloned.1.call-done
  113.6 69.1 %all-gather.6.cloned.1.call-done = bf16[2048,1024]{0,1:T(8,128)(2,1)} async-done(((bf16[256,1024]{0,1:T(8,128)(2,1)}), bf16[2048,1024]{0,1:T(8,128)(2,1)}) %all-gather.6.cloned.1.call-update) | async-done | bytes 4194320 | tf_op jit(solution)/shard_map/all_gather | solution.py:176
  182.7 6.5 copy.112
  195.5 49.0 %while.39 = (s32[]{:T(128)}, f32[16,256]{1,0:T(8,128)S(1)}, f32[16,256]{1,0:T(8,128)S(1)}, f32[256,16,64]{0,2,1:T(8,128)}, s32[1,256]{1,0:T(1,128)S(1)}, /*index...) while((s32[]{:T(128)}, f32[16,256]{1,0:T(8,128)S(1)}, ...), condition=%wide.region_8.9_spmd.clone, body=%wide.region_5.8_spmd.clone.sunk | while | flops 565075968 | bytes 43261180 | solution.py:50
  270.5 80.5 %while.40 = (s32[]{:T(128)}, f32[256,16,64]{0,2,1:T(8,128)}, bf16[4,512,1024]{1,2,0:T(8,128)(2,1)}, s32[1,256]{1,0:T(1,128)S(1)}, s32[4]{0:T(128)}, /*index=5*/s...) while((s32[]{:T(128)}, f32[256,16,64]{0,2,1:T(8,128)}, ...), condition=%wide.region_15.16_spmd.clone, body=%wide.region_14.15_spmd.clone.sunk | while | flops 818806784 | bytes 27565260 | solution.py:50
  282.6 8.2 fusion.216
  302.5 8.3 fusion.216
  322.6 8.3 fusion.216
  342.7 8.3 fusion.216
  353.9 6.4 copy.122
  360.3 30.6 %all_gather.27 = f32[16,2048]{1,0:T(8,128)S(1)} all-gather(f32[16,256]{1,0:T(8,128)S(1)} %get-tuple-element.1062), channel_id=1, replica_groups=mesh['rows'=4,'seq'=8] {'seq'}, dimensions={1}, use_global_device_ids=true | all-gather | bytes 147456 | tf_op jit(solution)/shard_map/all_gather | solution.py:215
  390.8 30.5 %all_gather.29 = f32[16,2048]{1,0:T(8,128)S(1)} all-gather(f32[16,256]{1,0:T(8,128)S(1)} %get-tuple-element.1061), channel_id=1, replica_groups=mesh['rows'=4,'seq'=8] {'seq'}, dimensions={1}, use_global_device_ids=true | all-gather | bytes 147456 | tf_op jit(solution)/shard_map/all_gather | solution.py:216
  421.3 123.6 %while.41 = (s32[]{:T(128)}, f32[256,16,64]{0,2,1:T(8,128)}, f32[256,16,64]{0,2,1:T(8,128)}, bf16[4,512,1024]{2,1,0:T(8,128)(2,1)}, s32[4]{0:T(128)}, /*index=5*...) while((s32[]{:T(128)}, f32[256,16,64]{0,2,1:T(8,128)}, ...), condition=%wide.region_17.18_spmd.clone, body=%wide.region_16.17_spmd.clone.sunk | while | flops 1096155136 | bytes 44670224 | solution.py:50
  437.7 8.5 fusion.225
  468.2 8.7 fusion.225
  499.1 8.7 fusion.225
  530.1 8.7 fusion.225
  612.3 6.4 fusion.93
  626.3 10.3 fusion.78
  636.6 10.2 fusion.71
  646.8 26.3 %add_add_fusion = f32[1024,6144]{1,0:T(8,128)} fusion(f32[1024,6144]{1,0:T(8,128)} %fusion.71, f32[1024,6144]{1,0:T(8,128)} %fusion.78, bf16[32,1024]{1,0:T(8,128)(2,1)S(1)} %copy-done.27, f32[32,6144]{1,0:T(8,128)S(1)} %get-tuple-element.658), kind=kOutput, calls=%fused_computation.57 | convolution fusion | flops 416612352 | bytes 76349440 | tf_op jit(solution)/shard_map/dot_general | solution.py:329
  678.9 38.4 %all-reduce.8 = (f32[1024]{0:T(1024)S(1)}, f32[6144]{0:T(1024)S(1)}, f32[1024]{0:T(1024)S(1)}, f32[1024]{0:T(1024)S(1)}, f32[1024]{0:T(1024)S(1)}, /*index=5*/f3...) all-reduce(f32[1024]{0:T(1024)S(1)} %get-tuple-element.605, ...), channel_id=5, replica_groups=mesh['rows'=4,'seq'=8] {'rows','seq'}, use_global_device_ids=true, to_apply=%region_23.24.clone | all-reduce | flops 14336 | bytes 114688
  725.5 141.4 %reduce-scatter.22.cloned.1.call-done = f32[32,1024]{1,0:T(8,128)} async-done(((f32[1024,1024]{1,0:T(8,128)}), f32[32,1024]{1,0:T(8,128)}) %reduce-scatter.22.cloned.1.call-update) | async-done | bytes 131088 | tf_op jit(solution)/shard_map/reduce_scatter | solution.py:365
  866.9 106.6 %reduce-scatter.12.cloned.1.call-done = f32[712,32]{0,1:T(8,128)} async-done(((f32[712,1024]{0,1:T(8,128)}), f32[712,32]{0,1:T(8,128)}) %reduce-scatter.12.cloned.1.call-update) | async-done | bytes 91152 | tf_op jit(solution)/shard_map/reduce_scatter | solution.py:355
  973.5 145.8 %reduce-scatter.18.cloned.1.call-done = f32[32,1024]{1,0:T(8,128)} async-done(((f32[1024,1024]{1,0:T(8,128)}), f32[32,1024]{1,0:T(8,128)}) %reduce-scatter.18.cloned.1.call-update) | async-done | bytes 131088 | tf_op jit(solution)/shard_map/reduce_scatter | solution.py:361
  1119.4 144.7 %reduce-scatter.16.cloned.1.call-done = f32[32,1024]{1,0:T(8,128)} async-done(((f32[1024,1024]{1,0:T(8,128)}), f32[32,1024]{1,0:T(8,128)}) %reduce-scatter.16.cloned.1.call-update) | async-done | bytes 131088 | tf_op jit(solution)/shard_map/reduce_scatter | solution.py:359
  1264.0 144.8 %reduce-scatter.20.cloned.1.call-done = f32[32,1024]{1,0:T(8,128)} async-done(((f32[1024,1024]{1,0:T(8,128)}), f32[32,1024]{1,0:T(8,128)}) %reduce-scatter.20.cloned.1.call-update) | async-done | bytes 131088 | tf_op jit(solution)/shard_map/reduce_scatter | solution.py:363
  1408.9 184.4 %reduce-scatter.26.cloned.1.call-done = f32[64,1024]{1,0:T(8,128)} async-done(((f32[2048,1024]{1,0:T(8,128)}), f32[64,1024]{1,0:T(8,128)}) %reduce-scatter.26.cloned.1.call-update) | async-done | bytes 262160 | tf_op jit(solution)/shard_map/reduce_scatter | solution.py:369
  1593.3 187.2 %reduce-scatter.24.cloned.1.call-done = f32[32,2048]{1,0:T(8,128)} async-done(((f32[1024,2048]{1,0:T(8,128)}), f32[32,2048]{1,0:T(8,128)}) %reduce-scatter.24.cloned.1.call-update) | async-done | bytes 262160 | tf_op jit(solution)/shard_map/reduce_scatter | solution.py:367
  1780.4 253.3 %reduce-scatter.14.cloned.1.call-done = f32[32,6144]{1,0:T(8,128)} async-done(((f32[1024,6144]{1,0:T(8,128)}), f32[32,6144]{1,0:T(8,128)}) %reduce-scatter.14.cloned.1.call-update) | async-done | bytes 786448 | tf_op jit(solution)/shard_map/reduce_scatter | solution.py:357
  (423 shorter events, 348.1 us)
Async XLA Ops:
  7.2 22.2 %copy-start = (bf16[1024,1024]{1,0:T(8,128)(2,1)S(1)}, bf16[1024,1024]{1,0:T(8,128)(2,1)}, u32[]{:S(2)}) copy-start(bf16[1024,1024]{1,0:T(8,128)(2,1)} %param.47) | copy-start | bytes 6291460
  7.2 8.8 copy-start.54
  7.2 100.1 %all-gather.8.cloned.1.call-start = ((), (), s32[]{:S(2)}) async-start(), calls=%async_computation.10 | async-start | bytes 4718592 | tf_op jit(solution)/shard_map/all_gather | solution.py:177
  8.4 14.5 copy-start.26
  9.3 13.5 copy-start.45
  11.1 11.8 copy-start.66
  15.1 230.8 %copy-start.2 = (f32[256,1024]{1,0:T(8,128)}, f32[256,1024]{1,0:T(8,128)S(1)}, u32[]{:S(2)}) copy-start(f32[256,1024]{1,0:T(8,128)S(1)} %get-tuple-element.651) | copy-start | bytes 3145732
  15.1 10.5 copy-start.52
  16.0 9.6 copy-start.60
  30.9 9.2 copy-start.76
  31.0 151.7 %all-gather.6.cloned.1.call-start = ((), (), s32[]{:S(2)}) async-start(), calls=%async_computation.9 | async-start | bytes 4718592 | tf_op jit(solution)/shard_map/all_gather | solution.py:176
  55.8 9.9 copy-start.42
  59.8 294.0 %all-gather.10.cloned.1.call-start = ((), (), s32[]{:S(2)}) async-start(), calls=%async_computation.11 | async-start | bytes 4718592 | tf_op jit(solution)/shard_map/all_gather | solution.py:290
  65.1 356.2 %all-gather.12.cloned.1.call-start = ((), (), s32[]{:S(2)}) async-start(), calls=%async_computation.12 | async-start | bytes 4718592 | tf_op jit(solution)/shard_map/all_gather | solution.py:291
  195.5 50.4 %copy-start.55 = (f32[1024]{0:T(1024)S(1)}, f32[1024]{0:T(1024)}, u32[]{:S(2)}) copy-start(f32[1024]{0:T(1024)} %param.50) | copy-start | bytes 12292
  245.8 7.6 copy-start.14
  249.7 12.7 copy-start.4
  250.0 12.5 copy-start.56
  269.2 454.9 %reduce-scatter.28.cloned.1.call-start = ((), (), s32[]{:S(2)}) async-start(), calls=%async_computation.21 | async-start | bytes 540672
  421.3 128.8 %copy-start.44 = (f32[256,32]{0,1:T(8,128)S(1)}, f32[256,32]{0,1:T(8,128)}, u32[]{:S(2)}) copy-start(f32[256,32]{0,1:T(8,128)} %copy-done.43) | copy-start | bytes 98308
  421.3 128.8 %copy-start.49 = (f32[256,32]{0,1:T(8,128)S(1)}, f32[256,32]{0,1:T(8,128)}, u32[]{:S(2)}) copy-start(f32[256,32]{0,1:T(8,128)} %get-tuple-element.643) | copy-start | bytes 98308
  421.6 6.7 copy-start.39
  547.0 21.5 %copy-start.16 = (bf16[256,16,64]{0,2,1:T(8,128)(2,1)}, bf16[256,16,64]{0,2,1:T(8,128)(2,1)S(1)}, u32[]{:S(2)}) copy-start(bf16[256,16,64]{0,2,1:T(8,128)(2,1)S(1)} %get-tuple-element.600) | copy-start | bytes 1572868
  570.9 7.6 slice-start
  591.2 275.7 %reduce-scatter.22.cloned.1.call-start = ((), (), s32[]{:S(2)}) async-start(), calls=%async_computation.18 | async-start | bytes 4325376 | tf_op jit(solution)/shard_map/reduce_scatter | solution.py:365
  595.1 378.5 %reduce-scatter.12.cloned.1.call-start = ((), (), s32[]{:S(2)}) async-start(), calls=%async_computation.13 | async-start | bytes 3244032 | tf_op jit(solution)/shard_map/reduce_scatter | solution.py:355
  599.5 519.8 %reduce-scatter.18.cloned.1.call-start = ((), (), s32[]{:S(2)}) async-start(), calls=%async_computation.16 | async-start | bytes 4325376 | tf_op jit(solution)/shard_map/reduce_scatter | solution.py:361
  603.4 660.6 %reduce-scatter.16.cloned.1.call-start = ((), (), s32[]{:S(2)}) async-start(), calls=%async_computation.15 | async-start | bytes 4325376 | tf_op jit(solution)/shard_map/reduce_scatter | solution.py:359
  607.4 801.5 %reduce-scatter.20.cloned.1.call-start = ((), (), s32[]{:S(2)}) async-start(), calls=%async_computation.17 | async-start | bytes 4325376 | tf_op jit(solution)/shard_map/reduce_scatter | solution.py:363
  611.2 982.0 %reduce-scatter.26.cloned.1.call-start = ((), (), s32[]{:S(2)}) async-start(), calls=%async_computation.20 | async-start | bytes 8650752 | tf_op jit(solution)/shard_map/reduce_scatter | solution.py:369
  618.7 1161.8 %reduce-scatter.24.cloned.1.call-start = ((), (), s32[]{:S(2)}) async-start(), calls=%async_computation.19 | async-start | bytes 8650752 | tf_op jit(solution)/shard_map/reduce_scatter | solution.py:367
  625.5 1408.3 %reduce-scatter.14.cloned.1.call-start = ((), (), s32[]{:S(2)}) async-start(), calls=%async_computation.14 | async-start | bytes 25952256 | tf_op jit(solution)/shard_map/reduce_scatter | solution.py:357
  (76 other events, 242.9 us)
Sparse Core Ops, SparseCore 0:
  31.1 76.2 all-gather.7
  109.4 73.2 all-gather.5
  184.8 73.2 all-gather.9
  269.3 71.6 all-gather.11
  591.3 132.7 reduce-scatter.27
  726.9 139.9 reduce-scatter.21
  873.8 99.7 reduce-scatter.11
  976.5 142.8 reduce-scatter.17
  1122.3 141.6 reduce-scatter.15
  1266.8 141.9 reduce-scatter.19
  1411.8 181.3 reduce-scatter.25
  1596.1 184.2 reduce-scatter.23
  1788.6 245.1 reduce-scatter.13
where the time goes:
time: 2050 us; the launch traced here: 2040 us
  waiting for transfers between devices  1390 us (68%)
  matrix products  292 us (14%)
  local copies, waits for them, and re-layouts  143 us (7%)
  blocking collectives  122 us (6%)
  other arithmetic  51.2 us (2%)
  loops' own time  24.8 us (1%)
    reduce_scatter x1, waiting for transfers between devices, shards(): lax.psum_scatter(part_w_ada, ('rows', 'seq'), scatter_dimension=0, tiled=...  253 us
    reduce_scatter x1, waiting for transfers between devices, shards(): lax.psum_scatter(part_w_up, ('rows', 'seq'), scatter_dimension=0, tiled=T...  187 us
    reduce_scatter x1, waiting for transfers between devices, shards(): lax.psum_scatter(part_w_down, ('rows', 'seq'), scatter_dimension=0, tiled...  184 us
    reduce_scatter x1, waiting for transfers between devices, shards(): lax.psum_scatter(part_w_key, ('rows', 'seq'), scatter_dimension=0, tiled=...  146 us
    reduce_scatter x1, waiting for transfers between devices, shards(): lax.psum_scatter(part_w_value, ('rows', 'seq'), scatter_dimension=0, tile...  145 us
    reduce_scatter x1, waiting for transfers between devices, shards(): lax.psum_scatter(part_w_query, ('rows', 'seq'), scatter_dimension=0, tile...  145 us
    reduce_scatter x1, waiting for transfers between devices, shards(): lax.psum_scatter(part_w_out, ('rows', 'seq'), scatter_dimension=0, tiled=...  141 us
    reduce_scatter x1, waiting for transfers between devices, shards(): lax.psum_scatter(part_w_input, ('rows', 'seq'), scatter_dimension=1, tile...  107 us
  transfers between devices with their start and end apart: 13, of which 11 were waited for; matrix products, arithmetic and copies ran while one was open for 14% of the time, Pallas kernels for 0%

commit v1 on v0

--- a/solution.py
+++ b/solution.py
@@ -1,11 +1,1217 @@
+import functools
 import math
 
 import jax
 import jax.numpy as jnp
+import numpy as np
 from jax import lax
+from jax.experimental import pallas as pl
+from jax.experimental.pallas import tpu as pltpu
 from jax.sharding import PartitionSpec as P
 
 HEADS = 16
+LANES = 128
+FAR = 1e30
+MESH = pl.DeviceIdType.MESH
+f32 = jnp.float32
+bf16 = jnp.bfloat16
+VMEM_BYTES = 60 * 2**20
+
+
+def dot(left, right):
+    return jnp.dot(left, right, preferred_element_type=f32)
+
+
+def dot_nt(left, right):
+    return lax.dot_general(left, right, (((1,), (1,)), ((), ())), preferred_element_type=f32)
+
+
+def remote(src, dst, send_sem, recv_sem, device):
+    return pltpu.make_async_remote_copy(
+        src_ref=src, dst_ref=dst, send_sem=send_sem, recv_sem=recv_sem, device_id=device, device_id_type=MESH
+    )
+
+
+def greet(devices):
+    barrier = pltpu.get_barrier_semaphore()
+    for device in devices:
+        pl.semaphore_signal(barrier, inc=1, device_id=device, device_id_type=MESH)
+    pl.semaphore_wait(barrier, len(devices))
+
+
+def other(value):
+    return value + 1 - 2 * (value % 2)
+
+
+def bit_partner(bit, row, seq):
+    if bit == "core":
+        return (other(row), seq)
+    if bit == "x":
+        return ((row + 2) % 4, seq)
+    if bit == "y":
+        return (row, other(seq))
+    if bit == "z0":
+        return (row, seq + 2 - 4 * ((seq // 2) % 2))
+    return (row, (seq + 4) % 8)
+
+
+def bit_value(bit, row, seq):
+    return {"core": row % 2, "x": row // 2, "y": seq % 2, "z0": (seq // 2) % 2, "z1": seq // 4}[bit]
+
+
+def place_of(order, shard):
+    row, seq = shard // 8, shard % 8
+    return sum(int(bit_value(bit, row, seq)) << (len(order) - 1 - at) for at, bit in enumerate(order))
+
+
+class Halving:
+    def __init__(self, order, held, landed, send_sems, recv_sems, row, seq):
+        self.order, self.held, self.landed = order, held, landed
+        self.send_sems, self.recv_sems = send_sems, recv_sems
+        self.row, self.seq = row, seq
+        self.offset, self.size, self.base, self.stage = 0, held.shape[0], 0, 0
+        self.copies = []
+
+    def send(self):
+        bit = self.order[self.stage]
+        half = self.size // 2
+        mine = bit_value(bit, self.row, self.seq)
+        copy = remote(
+            self.held.at[pl.ds(self.offset + (1 - mine) * half, half)],
+            self.landed.at[pl.ds(self.base, half)],
+            self.send_sems.at[self.stage],
+            self.recv_sems.at[self.stage],
+            bit_partner(bit, self.row, self.seq),
+        )
+        copy.start()
+        self.copies.append(copy)
+        self.offset = self.offset + mine * half
+        self.size = half
+        self.stage += 1
+
+    def add(self, out=None):
+        self.copies[-1].wait_recv()
+        offset, base = self.offset, self.base
+
+        def one(at, carried):
+            total = self.held[offset + at].astype(f32) + self.landed[base + at].astype(f32)
+            if out is None:
+                self.held[offset + at] = total.astype(bf16)
+            else:
+                out[...] = total
+            return carried
+
+        lax.fori_loop(0, self.size, one, 0)
+        self.base += self.size
+
+    def finish(self):
+        for copy in self.copies:
+            copy.wait_send()
+
+
+def by_segment(seg, table):
+    count = table.shape[0]
+    spread = table[count - 1 :]
+    for at in reversed(range(count - 1)):
+        spread = jnp.where(seg <= at, table[at : at + 1], spread)
+    return spread
+
+
+def normed(values):
+    centred = values - jnp.mean(values, axis=1, keepdims=True)
+    scale = lax.rsqrt(jnp.mean(centred * centred, axis=1, keepdims=True) + 1e-06)
+    return centred * scale, scale
+
+
+def norm_back(norm, scale, grad):
+    return (
+        grad - jnp.mean(grad, axis=1, keepdims=True) - norm * jnp.mean(grad * norm, axis=1, keepdims=True)
+    ) * scale
+
+
+def eights(values):
+    return jnp.sum(values.reshape(values.shape[0] // 8, 8, values.shape[1]), axis=0)
+
+
+def add_segments(sums, seg, values):
+    for at in range(sums.shape[0]):
+        sums[at] += eights(jnp.where(seg == at, values, 0.0))
+
+
+def turn(values, cosine, sine):
+    lane = lax.broadcasted_iota(jnp.int32, values.shape, 1)
+    swapped = jnp.where(lane % 2 == 0, pltpu.roll(values, LANES - 1, 1), pltpu.roll(values, 1, 1))
+    return values * cosine + swapped * sine
+
+
+def parts_of(values):
+    first = values.astype(bf16).astype(f32)
+    second = (values - first).astype(bf16).astype(f32)
+    return first, second, values - first - second
+
+
+def row_loop(count, step, body):
+    def one(at, carried):
+        body(pl.ds(pl.multiple_of(at * step, step), step))
+        return carried
+
+    lax.fori_loop(0, count // step, one, 0)
+
+def embed_kernel(
+    noisy, cond, text, seg_in, drop_cond, drop_text, time_index, table, w_input, b_input, w_ada, b_ada,
+    mod, stream, attn_in, features, silu, shift_scale, packed,
+):
+    step = pl.program_id(0)
+    segments = drop_cond.shape[1]
+    width = stream.shape[1]
+    frames = stream.shape[0]
+
+    @pl.when(step == 0)
+    def _():
+        picked = [table[pl.ds(time_index[0, at], 1), :] for at in range(segments)]
+        picked = jnp.concatenate(picked + [jnp.zeros((16 - segments, width), f32)], axis=0)
+        silu[...] = (picked / (1.0 + jnp.exp(-picked))).astype(bf16)
+        seg = seg_in[...]
+        keep_cond = jnp.zeros((frames, 1), f32)
+        keep_text = jnp.zeros((frames, 1), f32)
+        for at in range(segments):
+            keep_cond = jnp.where(seg == at, (1 - drop_cond[0, at]).astype(f32), keep_cond)
+            keep_text = jnp.where(seg == at, (1 - drop_text[0, at]).astype(f32), keep_text)
+        mel = noisy.shape[1]
+        packed[...] = jnp.concatenate(
+            [
+                noisy[...].astype(f32),
+                cond[...].astype(f32) * keep_cond,
+                text[...].astype(f32) * keep_text,
+                jnp.zeros((frames, packed.shape[1] - 2 * mel - text.shape[1]), f32),
+            ],
+            axis=1,
+        )
+        features[...] = packed[...].astype(bf16)
+        stream[...] = dot(features[:, : w_input.shape[0]], w_input[...]) + b_input[...]
+
+    block = dot(silu[...], w_ada[...])[:8] + b_ada[...]
+    mod[...] = block
+
+    @pl.when(step < 2)
+    def _():
+        shift_scale[step] = block
+
+    @pl.when(step == 1)
+    def _():
+        def rows(at):
+            seg = seg_in[at, :]
+            norm, unused = normed(stream[at, :])
+            shift = by_segment(seg, shift_scale[0, :segments])
+            scale = by_segment(seg, shift_scale[1, :segments])
+            attn_in[at, :] = (norm * (1.0 + scale) + shift).astype(bf16)
+
+        row_loop(frames, 32, rows)
+
+
+def embed(noisy, cond, text, seg, drop_cond, drop_text, time_index, table, w_input, b_input, w_ada, b_ada):
+    frames = noisy.shape[0]
+    width = w_input.shape[1]
+    blocks = w_ada.shape[1] // width
+    padded = -(-w_input.shape[0] // LANES) * LANES
+    whole = lambda array: pl.BlockSpec(array.shape, lambda j: (0,) * array.ndim)
+    scalar = pl.BlockSpec(memory_space=pltpu.SMEM)
+    return pl.pallas_call(
+        embed_kernel,
+        grid=(blocks,),
+        out_shape=(
+            jax.ShapeDtypeStruct((8, w_ada.shape[1]), f32),
+            jax.ShapeDtypeStruct((frames, width), f32),
+            jax.ShapeDtypeStruct((frames, width), bf16),
+            jax.ShapeDtypeStruct((frames, padded), bf16),
+        ),
+        in_specs=[
+            whole(noisy), whole(cond), whole(text), whole(seg), scalar, scalar, scalar, whole(table), whole(w_input),
+            whole(b_input), pl.BlockSpec((width, width), lambda j: (0, j)), pl.BlockSpec((1, width), lambda j: (0, j)),
+        ],
+        out_specs=(
+            pl.BlockSpec((8, width), lambda j: (0, j)),
+            pl.BlockSpec((frames, width), lambda j: (0, 0)),
+            pl.BlockSpec((frames, width), lambda j: (0, 0)),
+            pl.BlockSpec((frames, padded), lambda j: (0, 0)),
+        ),
+        scratch_shapes=[
+            pltpu.VMEM((16, width), bf16),
+            pltpu.VMEM((2, 8, width), f32),
+            pltpu.VMEM((frames, padded), f32),
+        ],
+        compiler_params=pltpu.CompilerParams(vmem_limit_bytes=VMEM_BYTES),
+        name="embed",
+    )(noisy, cond, text, seg, drop_cond, drop_text, time_index, table, w_input, b_input, w_ada, b_ada)
+
+
+def attend_kernel(
+    segments, x_in, onehot, w_query, w_key, w_value, b_query, b_key, b_value, cosine, sine,
+    att, x_all, query, key, value, attended,
+    w_three, value_one, onehots, out_tiles,
+    w_sems, own_sem, up_sems, down_sems, cross_sems, x_sems, hot_send, hot_recv, out_send, out_recv,
+):
+    row, seq = lax.axis_index("rows"), lax.axis_index("seq")
+    frames = x_in.shape[0]
+    peers = query.shape[1] // frames
+    depth = peers // 2
+    high, low = seq // 2, seq % 2
+    mine = pl.ds(pl.multiple_of(seq * LANES, LANES), LANES)
+    block_rows = lambda at: pl.ds(pl.multiple_of(at * frames, frames), frames)
+
+    loads = []
+    for at, weight in enumerate((w_query, w_key, w_value)):
+        load = pltpu.make_async_copy(weight.at[:, mine], w_three.at[:, pl.ds(at * LANES, LANES)], w_sems.at[at])
+        load.start()
+        loads.append(load)
+    own = pltpu.make_async_copy(x_in, x_all.at[block_rows(seq)], own_sem)
+    own.start()
+    greet([(row, lax.rem(seq + ahead, peers)) for ahead in range(1, peers)])
+
+    hot_copies = []
+    for ahead in range(1, peers):
+        copy = remote(
+            onehot, onehots.at[seq], hot_send.at[ahead], hot_recv.at[seq], (row, lax.rem(seq + ahead, peers))
+        )
+        copy.start()
+        hot_copies.append(copy)
+    onehots[seq] = onehot[...]
+    own.wait()
+
+    def hop(block, sems, device):
+        rows = x_all.at[block_rows(block)]
+        return remote(rows, rows, sems.at[block], x_sems.at[block], device)
+
+    def up(block):
+        return hop(block, up_sems, (row, seq + 2))
+
+    def down(block):
+        return hop(block, down_sems, (row, seq - 2))
+
+    def cross(block):
+        return hop(block, cross_sems, (row, other(seq)))
+
+    def arrived(block):
+        cross(block).wait_recv()
+
+    lane = lax.broadcasted_iota(jnp.int32, (frames, LANES), 1)
+
+    def project(block):
+        rows = block_rows(block)
+        three = dot(x_all[rows, :], w_three[...])
+        turns = cosine[rows, :], sine[rows, :]
+        rotated = turn(three[:, :LANES] + b_query[:, mine], *turns).astype(bf16).astype(f32) * 0.125
+        extras = jnp.concatenate([onehots[block], jnp.zeros((LANES - 8, frames), f32)], axis=0).T
+        walls = jnp.where(lane < segments, (extras - 1.0) * FAR, 0.0).astype(bf16)
+        for head in range(2):
+            query[head, rows, :LANES] = jnp.where(lane // 64 == head, rotated, 0.0).astype(bf16)
+            query[head, rows, LANES:] = walls
+        key[rows, :LANES] = turn(three[:, LANES : 2 * LANES] + b_key[:, mine], *turns).astype(bf16)
+        key[rows, LANES:] = extras.astype(bf16)
+        values = (three[:, 2 * LANES :] + b_value[:, mine]).astype(bf16)
+        value[rows, :] = values
+        value_one[rows, :LANES] = values
+        value_one[rows, LANES:] = jnp.ones((frames, LANES), bf16)
+
+    for load in loads:
+        load.wait()
+    for copy in hot_copies:
+        copy.wait_send()
+    for ahead in range(1, peers):
+        source = lax.rem(seq + peers - ahead, peers)
+        remote(onehot, onehots.at[source], hot_send.at[0], hot_recv.at[source], (row, source)).wait_recv()
+
+    @pl.when(high < depth - 1)
+    def _():
+        up(seq).start()
+
+    @pl.when(high > 0)
+    def _():
+        down(seq).start()
+
+    cross(seq).start()
+    project(seq)
+
+    def ring(step, carried):
+        from_low, from_high = seq - 2 * step, seq + 2 * step
+
+        @pl.when(from_low >= 0)
+        def _():
+            arrived(from_low)
+
+            @pl.when(high < depth - 1)
+            def _():
+                up(from_low).start()
+
+            cross(from_low).start()
+
+        @pl.when(from_high < peers)
+        def _():
+            arrived(from_high)
+
+            @pl.when(high > 0)
+            def _():
+                down(from_high).start()
+
+            cross(from_high).start()
+
+        @pl.when(from_low >= 0)
+        def _():
+            project(from_low)
+
+        @pl.when(from_high < peers)
+        def _():
+            project(from_high)
+
+        return carried
+
+    lax.fori_loop(1, depth, ring, 0)
+
+    def crossed(step, carried):
+        block = 2 * lax.rem(high + step, depth) + 1 - low
+        arrived(block)
+        project(block)
+        return carried
+
+    lax.fori_loop(0, depth, crossed, 0)
+
+    def attend(step, carried):
+        block = lax.rem(seq + 1 + step, peers)
+        rows = block_rows(block)
+        outs = []
+        for head in range(2):
+            scores = dot_nt(query[head, rows, :], key[...])
+            top = jnp.max(scores, axis=1, keepdims=True)
+            weights = jnp.exp(scores - top).astype(bf16)
+            both = dot(weights, value_one[...])
+            total = both[:, LANES:]
+            outs.append(both[:, :LANES] / total)
+            first, second, third = parts_of(top + jnp.log(total))
+            extras = query[head, rows, LANES:].astype(f32)
+            extras = jnp.where(lane == segments, -first, extras)
+            extras = jnp.where(lane == segments + 1, -second, extras)
+            query[head, rows, LANES:] = jnp.where(lane == segments + 2, -third, extras).astype(bf16)
+        out = jnp.where(lane < 64, outs[0], outs[1])
+        attended[rows, :] = out
+        out_tiles[block] = out.astype(bf16)
+
+        @pl.when(step < peers - 1)
+        def _():
+            remote(out_tiles.at[block], att.at[:, mine], out_send.at[block], out_recv.at[seq], (row, block)).start()
+
+        return carried
+
+    lax.fori_loop(0, peers, attend, 0)
+    att[:, mine] = out_tiles[seq]
+
+    def finish(step, carried):
+        peer = lax.rem(seq + step, peers)
+        place = pl.ds(pl.multiple_of(peer * LANES, LANES), LANES)
+        copy = remote(out_tiles.at[peer], att.at[:, place], out_send.at[peer], out_recv.at[peer], (row, peer))
+        copy.wait_send()
+        copy.wait_recv()
+        return carried
+
+    lax.fori_loop(1, peers, finish, 0)
+
+    def sent(step, carried):
+        from_low, from_high = seq - 2 * step, seq + 2 * step
+
+        @pl.when(from_low >= 0)
+        def _():
+            @pl.when(high < depth - 1)
+            def _():
+                up(from_low).wait_send()
+
+            cross(from_low).wait_send()
+
+        @pl.when((from_high < peers) & (step > 0))
+        def _():
+            cross(from_high).wait_send()
+
+        @pl.when((from_high < peers) & (high > 0))
+        def _():
+            down(from_high).wait_send()
+
+        return carried
+
+    lax.fori_loop(0, depth, sent, 0)
+
+
+def attend(segments, peers, x_in, onehot, w_query, w_key, w_value, b_query, b_key, b_value, cosine, sine):
+    frames, width = x_in.shape
+    length = frames * peers
+    in_vmem = pl.BlockSpec(memory_space=pltpu.VMEM)
+    anywhere = pl.BlockSpec(memory_space=pl.ANY)
+    dma = pltpu.SemaphoreType.DMA
+    return pl.pallas_call(
+        functools.partial(attend_kernel, segments),
+        out_shape=(
+            jax.ShapeDtypeStruct((frames, width), bf16),
+            jax.ShapeDtypeStruct((length, width), bf16),
+            jax.ShapeDtypeStruct((2, length, 2 * LANES), bf16),
+            jax.ShapeDtypeStruct((length, 2 * LANES), bf16),
+            jax.ShapeDtypeStruct((length, LANES), bf16),
+            jax.ShapeDtypeStruct((length, LANES), f32),
+        ),
+        in_specs=[in_vmem, in_vmem, anywhere, anywhere, anywhere] + [in_vmem] * 5,
+        out_specs=(in_vmem,) * 6,
+        scratch_shapes=[
+            pltpu.VMEM((width, 3 * LANES), bf16),
+            pltpu.VMEM((length, 2 * LANES), bf16),
+            pltpu.VMEM((peers, 8, frames), f32),
+            pltpu.VMEM((peers, frames, LANES), bf16),
+            dma((3,)), dma, dma((peers,)), dma((peers,)), dma((peers,)), dma((peers,)),
+            dma((peers,)), dma((peers,)), dma((peers,)), dma((peers,)),
+        ],
+        compiler_params=pltpu.CompilerParams(collective_id=0, has_side_effects=True, vmem_limit_bytes=VMEM_BYTES),
+        name="attend",
+    )(x_in, onehot, w_query, w_key, w_value, b_query, b_key, b_value, cosine, sine)
+
+
+def feed_kernel(
+    segments, att, stream, mod, seg_in, cot, w_out, b_out, w_up, b_up, w_down, b_down,
+    layer_out, grad_middle, grad_att, act_t, grad_ffn, ffn_in_t, grad_up, att_t, grad_attn, sums, biases,
+    w_out_in, w_up_in, w_down_in, branch, middle, ffn_in, up_value, act, work, wide, seg_sums, bias_up, bias_side, sems,
+):
+    frames, width = att.shape
+    loads = []
+    for at, (src, dst) in enumerate(((w_out, w_out_in), (w_up, w_up_in), (w_down, w_down_in))):
+        load = pltpu.make_async_copy(src, dst, sems.at[at])
+        load.start()
+        loads.append(load)
+    seg_sums[...] = jnp.zeros_like(seg_sums)
+    bias_up[...] = jnp.zeros_like(bias_up)
+    bias_side[...] = jnp.zeros_like(bias_side)
+    part = lambda at: mod[:segments, at * width : (at + 1) * width]
+
+    loads[0].wait()
+    branch[...] = dot(att[...], w_out_in[...]) + b_out[...]
+
+    def join(rows):
+        seg = seg_in[rows, :]
+        here = stream[rows, :] + by_segment(seg, part(2)) * branch[rows, :]
+        middle[rows, :] = here
+        norm, unused = normed(here)
+        ffn_in[rows, :] = (norm * (1.0 + by_segment(seg, part(4))) + by_segment(seg, part(3))).astype(bf16)
+
+    row_loop(frames, 32, join)
+    loads[1].wait()
+    up_value[...] = dot(ffn_in[...], w_up_in[...]) + b_up[...]
+
+    def bend(rows):
+        value = up_value[rows, :]
+        curve = math.sqrt(2 / math.pi)
+        square = value * value
+        tanh = jnp.tanh(curve * value * (1.0 + 0.044715 * square))
+        half = 0.5 * (1.0 + tanh)
+        act[rows, :] = (value * half).astype(bf16)
+        up_value[rows, :] = half + 0.5 * value * (1.0 - tanh * tanh) * (curve * (1.0 + 3 * 0.044715 * square))
+
+    row_loop(frames, 16, bend)
+    loads[2].wait()
+    work[...] = dot(act[...], w_down_in[...]) + b_down[...]
+
+    def leave(rows):
+        seg = seg_in[rows, :]
+        gate = by_segment(seg, part(5))
+        grad = cot[rows, :].astype(f32)
+        ffn = work[rows, :]
+        layer_out[rows, :] = (middle[rows, :] + gate * ffn).astype(bf16)
+        down = (grad * gate).astype(bf16)
+        grad_ffn[rows, :] = down
+        bias_side[0] += eights(down.astype(f32))
+        add_segments(seg_sums.at[3], seg, grad * ffn)
+
+    row_loop(frames, 32, leave)
+    wide[...] = dot_nt(grad_ffn[...], w_down_in[...])
+
+    def unbend(rows):
+        up = (wide[rows, :] * up_value[rows, :]).astype(bf16)
+        grad_up[rows, :] = up
+        bias_up[...] += eights(up.astype(f32))
+
+    row_loop(frames, 32, unbend)
+    work[...] = dot_nt(grad_up[...], w_up_in[...])
+
+    def back(rows):
+        seg = seg_in[rows, :]
+        norm, scale = normed(middle[rows, :])
+        grad = work[rows, :]
+        add_segments(seg_sums.at[1], seg, grad)
+        add_segments(seg_sums.at[2], seg, grad * norm)
+        grad = norm_back(norm, scale, grad * (1.0 + by_segment(seg, part(4)))) + cot[rows, :].astype(f32)
+        grad_middle[rows, :] = grad
+        attn = (grad * by_segment(seg, part(2))).astype(bf16)
+        grad_attn[rows, :] = attn
+        bias_side[1] += eights(attn.astype(f32))
+        add_segments(seg_sums.at[0], seg, grad * branch[rows, :])
+
+    row_loop(frames, 32, back)
+    grad_att[...] = dot_nt(grad_attn[...], w_out_in[...]).astype(bf16)
+    act_t[...] = act[...].T
+    ffn_in_t[...] = ffn_in[...].T
+    att_t[...] = att[...].T
+    for at in range(4):
+        sums[at] = jnp.concatenate(
+            [jnp.sum(seg_sums[at, k], axis=0, keepdims=True) for k in range(segments)]
+            + [jnp.zeros((8 - segments, width), f32)],
+            axis=0,
+        )
+    biases[:, :width] = jnp.sum(bias_side[1], axis=0, keepdims=True)
+    biases[:, width:-width] = jnp.sum(bias_up[...], axis=0, keepdims=True)
+    biases[:, -width:] = jnp.sum(bias_side[0], axis=0, keepdims=True)
+
+
+def feed(segments, att, stream, mod, seg, cot, w_out, b_out, w_up, b_up, w_down, b_down):
+    frames, width = att.shape
+    hidden = w_up.shape[1]
+    in_vmem = pl.BlockSpec(memory_space=pltpu.VMEM)
+    anywhere = pl.BlockSpec(memory_space=pl.ANY)
+    shape = jax.ShapeDtypeStruct
+    return pl.pallas_call(
+        functools.partial(feed_kernel, segments),
+        out_shape=(
+            shape((frames, width), bf16),
+            shape((frames, width), f32),
+            shape((frames, width), bf16),
+            shape((hidden, frames), bf16),
+            shape((frames, width), bf16),
+            shape((width, frames), bf16),
+            shape((frames, hidden), bf16),
+            shape((width, frames), bf16),
+            shape((frames, width), bf16),
+            shape((4, 8, width), f32),
+            shape((1, hidden + 2 * width), f32),
+        ),
+        in_specs=[in_vmem] * 5 + [anywhere, in_vmem] * 3,
+        out_specs=(in_vmem,) * 11,
+        scratch_shapes=[
+            pltpu.VMEM(w_out.shape, bf16),
+            pltpu.VMEM(w_up.shape, bf16),
+            pltpu.VMEM(w_down.shape, bf16),
+            pltpu.VMEM((frames, width), f32),
+            pltpu.VMEM((frames, width), f32),
+            pltpu.VMEM((frames, width), bf16),
+            pltpu.VMEM((frames, hidden), f32),
+            pltpu.VMEM((frames, hidden), bf16),
+            pltpu.VMEM((frames, width), f32),
+            pltpu.VMEM((frames, hidden), f32),
+            pltpu.VMEM((4, segments, 8, width), f32),
+            pltpu.VMEM((8, hidden), f32),
+            pltpu.VMEM((2, 8, width), f32),
+            pltpu.SemaphoreType.DMA((3,)),
+        ],
+        compiler_params=pltpu.CompilerParams(vmem_limit_bytes=VMEM_BYTES),
+        name="feed",
+    )(att, stream, mod, seg, cot, w_out, b_out, w_up, b_up, w_down, b_down)
+
+
+CORE_FIRST = ("core", "x", "y", "z0", "z1")
+ACROSS_FIRST = ("core", "y", "x", "z0", "z1")
+
+
+def fill(held, order, left, right, columns):
+    rows = held.shape[1]
+    slab = 8 * rows
+    for at in range(4):
+        product = dot(left[at * slab : (at + 1) * slab, :], right[:, columns])
+        for inner in range(8):
+            held[place_of(order, at * 8 + inner)] = product[inner * rows : (inner + 1) * rows, :].astype(bf16)
+
+
+def return_kernel(
+    segments, grad_att, query, key, value, attended, x_all, cosine, sine,
+    act_t, grad_ffn, ffn_in_t, grad_up, att_t, grad_attn,
+    grads, grad_w_down, grad_w_up, grad_w_out, grad_w_three, grad_b_three,
+    grad_all, grad_low, value_ext, key_t, grad_query_t, tiles, grads_t,
+    held_a, held_b, held_c, held_d, held_e, land_a, land_b, land_c, land_d, land_e,
+    three_held, three_land, three_far, three_tiles, three_in,
+    do_send, do_recv, tile_send, tile_recv, half_send, half_recv, three_send, three_recv, last_send, last_recv,
+):
+    row, seq = lax.axis_index("rows"), lax.axis_index("seq")
+    frames = grad_att.shape[0]
+    width = grad_att.shape[1]
+    length = key.shape[0]
+    peers = length // frames
+    block_rows = lambda at: pl.ds(pl.multiple_of(at * frames, frames), frames)
+    columns_of = lambda at, which=0: pl.ds(pl.multiple_of(which * width + at * LANES, LANES), LANES)
+    core_partner = bit_partner("core", row, seq)
+    x_partner = bit_partner("x", row, seq)
+    greet([(row, lax.rem(seq + ahead, peers)) for ahead in range(1, peers)] + [core_partner, x_partner])
+
+    def tile_out(block):
+        return remote(
+            grad_att.at[:, columns_of(block)], grad_all.at[block_rows(seq)],
+            do_send.at[block], do_recv.at[seq], (row, block),
+        )
+
+    def start(step, carried):
+        tile_out(lax.rem(seq + step, peers)).start()
+        return carried
+
+    lax.fori_loop(1, peers, start, 0)
+    grad_all[block_rows(seq), :] = grad_att[:, columns_of(seq)]
+
+    chunks = []
+    plan = (
+        (held_a, land_a, CORE_FIRST, act_t, grad_ffn, slice(0, 512), grad_w_down.at[:, :512]),
+        (held_b, land_b, CORE_FIRST, act_t, grad_ffn, slice(512, 1024), grad_w_down.at[:, 512:]),
+        (held_c, land_c, ACROSS_FIRST, ffn_in_t, grad_up, slice(0, 1024), grad_w_up.at[:, :1024]),
+        (held_d, land_d, CORE_FIRST, ffn_in_t, grad_up, slice(1024, 2048), grad_w_up.at[:, 1024:]),
+        (held_e, land_e, ACROSS_FIRST, att_t, grad_attn, slice(0, 1024), grad_w_out),
+    )
+    for at, (held, land, order, left, right, columns, out) in enumerate(plan):
+        fill(held, order, left, right, columns)
+        chunk = Halving(order, held, land, half_send.at[at], half_recv.at[at], row, seq)
+        chunk.send()
+        chunks.append((chunk, out))
+
+    lane = lax.broadcasted_iota(jnp.int32, (frames, LANES), 1)
+
+    def prepare(step, carried):
+        block = lax.rem(seq + peers - step, peers)
+        rows = block_rows(block)
+
+        @pl.when(step > 0)
+        def _():
+            remote(
+                grad_att.at[:, columns_of(block)], grad_all.at[rows], do_send.at[block], do_recv.at[block], (row, block)
+            ).wait_recv()
+
+        grad = grad_all[rows, :].astype(f32)
+        product = grad * attended[rows, :]
+        for head in range(2):
+            inside = lane // 64 == head
+            first, second, third = parts_of(jnp.sum(jnp.where(inside, product, 0.0), axis=1, keepdims=True))
+            grad_low[head, rows, :LANES] = jnp.where(inside, grad, 0.0).astype(bf16)
+            extras = jnp.where(lane == segments, -first, 0.0)
+            extras = jnp.where(lane == segments + 1, -second, extras)
+            grad_low[head, rows, LANES:] = jnp.where(lane == segments + 2, -third, extras).astype(bf16)
+        value_ext[rows, :LANES] = value[rows, :]
+        value_ext[rows, LANES:] = key[rows, LANES:]
+        key_t[:, rows] = key[rows, :LANES].T
+        grad_query_t[:, rows] = jnp.zeros((LANES, frames), f32)
+        return carried
+
+    lax.fori_loop(0, peers, prepare, 0)
+    grad_b_three[...] = jnp.zeros_like(grad_b_three)
+
+    def hand_over(which, block, grad):
+        low = grad.astype(bf16)
+        tiles[which, block] = low
+        grads_t[which * LANES : (which + 1) * LANES, block_rows(block)] = low.T
+        grad_b_three[which : which + 1, :] += jnp.sum(low.astype(f32), axis=0, keepdims=True)
+
+    def tile_back(which, block):
+        return remote(
+            tiles.at[which, block], grads.at[:, columns_of(seq, which)],
+            tile_send.at[which, block], tile_recv.at[which, seq], (row, block),
+        )
+
+    span = min(512, length)
+
+    def key_block(step, carried):
+        block = lax.rem(seq + 1 + step, peers)
+        rows = block_rows(block)
+        keys, values = key[rows, :], value_ext[rows, :]
+        grad_key = jnp.zeros((frames, LANES), f32)
+        grad_value = jnp.zeros((frames, LANES), f32)
+        for at in range(length // span):
+            queries = slice(at * span, (at + 1) * span)
+            for head in range(2):
+                low = grad_low[head, queries, :]
+                ask = query[head, queries, :]
+                probs = jnp.exp(dot_nt(keys, ask))
+                grad_scores = (probs * dot_nt(values, low)).astype(bf16)
+                grad_value += dot(probs.astype(bf16), low[:, :LANES])
+                grad_key += dot(grad_scores, ask[:, :LANES])
+                half = slice(head * 64, (head + 1) * 64)
+                grad_query_t[half, queries] += dot(key_t[half, rows], grad_scores)
+        hand_over(1, block, turn(grad_key, cosine[rows, :], -sine[rows, :]))
+        hand_over(2, block, grad_value)
+
+        @pl.when(step < peers - 1)
+        def _():
+            tile_back(1, block).start()
+            tile_back(2, block).start()
+
+        for at, (chunk, out) in enumerate(chunks):
+            pass
+        return carried
+
+    lax.fori_loop(0, peers, key_block, 0)
+
+    def query_block(step, carried):
+        block = lax.rem(seq + 1 + step, peers)
+        rows = block_rows(block)
+        hand_over(0, block, turn(grad_query_t[:, rows].T * 0.125, cosine[rows, :], -sine[rows, :]))
+
+        @pl.when(step < peers - 1)
+        def _():
+            tile_back(0, block).start()
+
+        return carried
+
+    lax.fori_loop(0, peers, query_block, 0)
+    for which in range(3):
+        grads[:, columns_of(seq, which)] = tiles[which, seq]
+
+    three = dot(grads_t[...], x_all[...]).T
+    fourth = width // 4
+    for at in range(4):
+        place = (at % 2) * 2 + at // 2
+        three_held[place] = three[at * fourth : (at + 1) * fourth, :].astype(bf16)
+    core, x = row % 2, row // 2
+    first = remote(
+        three_held.at[pl.ds((1 - core) * 2, 2)], three_land, three_send.at[0], three_recv.at[0], core_partner
+    )
+    first.start()
+
+    for stage in range(5):
+        for chunk, out in chunks:
+            if stage < 4:
+                chunk.add()
+                chunk.send()
+            else:
+                chunk.add(out)
+        if stage == 0:
+            first.wait_recv()
+            for at in range(2):
+                total = three_held[core * 2 + at].astype(f32) + three_land[at].astype(f32)
+                three_held[core * 2 + at] = total.astype(bf16)
+            second = remote(
+                three_held.at[core * 2 + 1 - x], three_far, three_send.at[1], three_recv.at[1], x_partner
+            )
+            second.start()
+        if stage == 1:
+            second.wait_recv()
+            total = (three_held[core * 2 + x].astype(f32) + three_far[...].astype(f32)).astype(bf16)
+            slot = fourth // peers
+            for at in range(peers):
+                three_tiles[at] = total[at * slot : (at + 1) * slot, :]
+
+            def spread(block):
+                return remote(
+                    three_tiles.at[block], three_in.at[seq], last_send.at[block], last_recv.at[seq], (row, block)
+                )
+
+            def start_spread(step, carried):
+                spread(lax.rem(seq + step, peers)).start()
+                return carried
+
+            lax.fori_loop(1, peers, start_spread, 0)
+            three_in[seq] = three_tiles[seq]
+
+    def finish(step, carried):
+        peer = lax.rem(seq + step, peers)
+        tile_out(peer).wait_send()
+        for which in range(3):
+            copy = remote(
+                tiles.at[which, peer], grads.at[:, columns_of(peer, which)],
+                tile_send.at[which, peer], tile_recv.at[which, peer], (row, peer),
+            )
+            copy.wait_send()
+            copy.wait_recv()
+        copy = remote(three_tiles.at[peer], three_in.at[peer], last_send.at[peer], last_recv.at[peer], (row, peer))
+        copy.wait_send()
+        copy.wait_recv()
+        return carried
+
+    lax.fori_loop(1, peers, finish, 0)
+    for which in range(3):
+        for peer in range(peers):
+            grad_w_three[which, :, peer * LANES : (peer + 1) * LANES] = three_in[
+                peer, :, which * LANES : (which + 1) * LANES
+            ].astype(f32)
+    first.wait_send()
+    second.wait_send()
+    for chunk, out in chunks:
+        chunk.finish()
+
+
+def give_back(segments, grad_att, query, key, value, attended, x_all, cosine, sine, feeds):
+    frames, width = grad_att.shape
+    length = key.shape[0]
+    peers = length // frames
+    hidden = feeds[0].shape[0]
+    in_vmem = pl.BlockSpec(memory_space=pltpu.VMEM)
+    shape = jax.ShapeDtypeStruct
+    dma = pltpu.SemaphoreType.DMA
+    shards = 4 * peers
+    chunk_shapes = [
+        (shards, hidden // shards, width // 2),
+        (shards, hidden // shards, width // 2),
+        (shards, width // shards, hidden // 2),
+        (shards, width // shards, hidden // 2),
+        (shards, width // shards, width),
+    ]
+    return pl.pallas_call(
+        functools.partial(return_kernel, segments),
+        out_shape=(
+            shape((frames, 3 * width), bf16),
+            shape((hidden // shards, width), f32),
+            shape((width // shards, hidden), f32),
+            shape((width // shards, width), f32),
+            shape((3, width // shards, width), f32),
+            shape((8, LANES), f32),
+        ),
+        in_specs=[in_vmem] * 14,
+        out_specs=(in_vmem,) * 6,
+        scratch_shapes=[
+            pltpu.VMEM((length, LANES), bf16),
+            pltpu.VMEM((2, length, 2 * LANES), bf16),
+            pltpu.VMEM((length, 2 * LANES), bf16),
+            pltpu.VMEM((LANES, length), bf16),
+            pltpu.VMEM((LANES, length), f32),
+            pltpu.VMEM((3, peers, frames, LANES), bf16),
+            pltpu.VMEM((3 * LANES, length), bf16),
+        ]
+        + [pltpu.VMEM(dims, bf16) for dims in chunk_shapes]
+        + [pltpu.VMEM(dims, bf16) for dims in chunk_shapes]
+        + [
+            pltpu.VMEM((4, width // 4, 3 * LANES), bf16),
+            pltpu.VMEM((2, width // 4, 3 * LANES), bf16),
+            pltpu.VMEM((width // 4, 3 * LANES), bf16),
+            pltpu.VMEM((peers, width // shards, 3 * LANES), bf16),
+            pltpu.VMEM((peers, width // shards, 3 * LANES), bf16),
+            dma((peers,)), dma((peers,)), dma((3, peers)), dma((3, peers)), dma((5, 5)), dma((5, 5)),
+            dma((2,)), dma((2,)), dma((peers,)), dma((peers,)),
+        ],
+        compiler_params=pltpu.CompilerParams(collective_id=1, has_side_effects=True, vmem_limit_bytes=VMEM_BYTES),
+        name="give_back",
+    )(grad_att, query, key, value, attended, x_all, cosine, sine, *feeds)
+
+
+def close_kernel(
+    segments, mel, grads, stream, mod, seg_in, grad_middle, features, sums, bias_feed, bias_three, keeps, times, table,
+    table_mine, w_query, w_key, w_value, w_input, w_ada,
+    grad_features, grad_w_input, grad_w_ada, grad_table, small,
+    weights, ada_mine, grad_in, grad_stream, seg_sums, bias_sum, held_a, held_b, land_a, land_b, out_a, out_b,
+    packed, landed, gathered, mod_sums,
+    sems, half_send, half_recv, small_send, small_recv, wide_send, wide_recv,
+):
+    row, seq = lax.axis_index("rows"), lax.axis_index("seq")
+    frames, width = stream.shape
+    peers = packed.shape[0]
+    columns = mod.shape[1]
+    core_partner = bit_partner("core", row, seq)
+    x_partner = bit_partner("x", row, seq)
+    core, x = row % 2, row // 2
+
+    loads = []
+    for at, src in enumerate((w_query, w_key, w_value)):
+        load = pltpu.make_async_copy(src, weights.at[at], sems.at[at])
+        load.start()
+        loads.append(load)
+    slot = w_ada.shape[0] // (4 * peers)
+    ada_load = pltpu.make_async_copy(
+        w_ada.at[pl.ds(pl.multiple_of((row * peers + seq) * slot, slot), slot)], ada_mine, sems.at[3]
+    )
+    ada_load.start()
+    greet([(row, lax.rem(seq + ahead, peers)) for ahead in range(1, peers)] + [core_partner, x_partner])
+    seg_sums[...] = jnp.zeros_like(seg_sums)
+    bias_sum[...] = jnp.zeros_like(bias_sum)
+    for at, load in enumerate(loads):
+        load.wait()
+        product = dot_nt(grads[:, at * width : (at + 1) * width], weights[at])
+        grad_in[...] = product if at == 0 else grad_in[...] + product
+
+    def back(rows):
+        seg = seg_in[rows, :]
+        norm, scale = normed(stream[rows, :])
+        grad = grad_in[rows, :]
+        add_segments(seg_sums.at[0], seg, grad)
+        add_segments(seg_sums.at[1], seg, grad * norm)
+        spread = 1.0 + by_segment(seg, mod[:segments, width : 2 * width])
+        low = (grad_middle[rows, :] + norm_back(norm, scale, grad * spread)).astype(bf16)
+        grad_stream[rows, :] = low
+        bias_sum[...] += eights(low.astype(f32))
+
+    row_loop(frames, 32, back)
+    grad_t = grad_stream[...].T
+    half = features.shape[1] // 2
+    chunks = []
+    plan = ((held_a, land_a, CORE_FIRST, slice(0, half), out_a), (held_b, land_b, ACROSS_FIRST, slice(half, None), out_b))
+    for at, (held, land, order, some, out) in enumerate(plan):
+        fill(held, order, grad_t, features, some)
+        chunk = Halving(order, held, land, half_send.at[at], half_recv.at[at], row, seq)
+        chunk.send()
+        chunks.append((chunk, out))
+
+    piece = columns // peers // 2
+    for part in range(6):
+        source = seg_sums.at[part] if part < 2 else None
+        if source is not None:
+            rows4 = [jnp.sum(source[k], axis=0, keepdims=True) for k in range(segments)]
+            whole = jnp.concatenate(rows4 + [jnp.zeros((8 - segments, width), f32)], axis=0)
+        else:
+            whole = sums[part - 2]
+        mod_sums[:8, part * width : (part + 1) * width] = whole
+    for at in range(peers):
+        packed[at, :4, :piece] = mod_sums[:4, 2 * at * piece : (2 * at + 1) * piece]
+        packed[at, 4:, :piece] = mod_sums[:4, (2 * at + 1) * piece : (2 * at + 2) * piece]
+    tail = slice(piece, piece + LANES)
+
+    def eight_rows(values):
+        return jnp.concatenate([values[:, at * LANES : (at + 1) * LANES] for at in range(8)], axis=0)
+
+    for which in range(3):
+        picked = lax.broadcasted_iota(jnp.int32, (8, LANES), 0) == seq
+        packed[which, :, tail] = jnp.where(picked, bias_three[which : which + 1, :], 0.0)
+    for at in range(4):
+        packed[3 + at, :, tail] = eight_rows(bias_feed[:, at * width : (at + 1) * width])
+    packed[7, :, tail] = eight_rows(jnp.sum(bias_sum[...], axis=0, keepdims=True))
+
+    def small_out(block):
+        return remote(
+            packed.at[block], landed.at[seq], small_send.at[block], small_recv.at[seq], (row, block)
+        )
+
+    def start_small(step, carried):
+        small_out(lax.rem(seq + step, peers)).start()
+        return carried
+
+    lax.fori_loop(1, peers, start_small, 0)
+
+    grad = dot_nt(grad_stream[...], w_input[...])
+    lanes = lax.broadcasted_iota(jnp.int32, grad.shape, 1)
+    kept = jnp.where(lanes < mel, 1.0, jnp.where(lanes < 2 * mel, keeps[:, 0:1], keeps[:, 1:2]))
+    grad_features[...] = grad * kept
+
+    landed[seq] = packed[seq]
+
+    def wait_small(step, carried):
+        peer = lax.rem(seq + step, peers)
+        remote(packed.at[peer], landed.at[peer], small_send.at[peer], small_recv.at[peer], (row, peer)).wait_recv()
+        return carried
+
+    lax.fori_loop(1, peers, wait_small, 0)
+    gathered[core, seq, x, :, : piece + LANES] = jnp.sum(landed[...], axis=0)
+    gathered[core, seq, x, :, piece + LANES :] = times[...]
+    mine = gathered.at[core, seq, x]
+    to_x = remote(mine, mine, wide_send.at[peers], wide_recv.at[peers], x_partner)
+    to_x.start()
+    for chunk, out in chunks:
+        chunk.add()
+        chunk.send()
+    to_x.wait_recv()
+
+    def wide_out(block, source):
+        here = gathered.at[core, source]
+        return remote(here, here, wide_send.at[block], wide_recv.at[source], (row, block))
+
+    def start_wide(step, carried):
+        wide_out(lax.rem(seq + step, peers), seq).start()
+        return carried
+
+    lax.fori_loop(1, peers, start_wide, 0)
+    for chunk, out in chunks:
+        chunk.add()
+        chunk.send()
+
+    def wait_wide(step, carried):
+        peer = lax.rem(seq + step, peers)
+        wide_out(peer, peer).wait_recv()
+        return carried
+
+    lax.fori_loop(1, peers, wait_wide, 0)
+    to_core = remote(
+        gathered.at[core], gathered.at[core], wide_send.at[peers + 1], wide_recv.at[peers + 1], core_partner
+    )
+    to_core.start()
+    for chunk, out in chunks:
+        chunk.add()
+        chunk.send()
+    to_core.wait_recv()
+    for chunk, out in chunks:
+        chunk.add()
+        chunk.send()
+
+    for at in range(peers):
+        for other_row in range(4):
+            block = gathered[other_row % 2, at, other_row // 2]
+            mod_sums[other_row * 4 : other_row * 4 + 4, 2 * at * piece : (2 * at + 1) * piece] = block[:4, :piece]
+            mod_sums[other_row * 4 : other_row * 4 + 4, (2 * at + 1) * piece : (2 * at + 2) * piece] = block[4:, :piece]
+    picks = jnp.concatenate(
+        [gathered[r % 2, 0, r // 2, :4, piece + LANES : piece + LANES + table.shape[0]] for r in range(4)], axis=0
+    )
+    total = mod_sums[...]
+    exact = lax.Precision.HIGHEST
+    silu = table_mine[...] / (1.0 + jnp.exp(-table_mine[...]))
+    silu_low = silu.astype(bf16).astype(f32)
+    chosen = jnp.dot(picks, silu_low, precision=exact, preferred_element_type=f32)
+    three = [piece_of.astype(bf16) for piece_of in parts_of(total)]
+    left = chosen.T.astype(bf16)
+    grad_w_ada[...] = dot(left, three[0]) + dot(left, three[1]) + dot(left, three[2])
+    ada_load.wait()
+    ada = ada_mine[...]
+    back_sums = dot_nt(three[0], ada) + dot_nt(three[1], ada) + dot_nt(three[2], ada)
+    slope = 1.0 / (1.0 + jnp.exp(-table_mine[...]))
+    slope = slope * (1.0 + table_mine[...] * (1.0 - slope))
+    grad_table[...] = jnp.dot(picks.T, back_sums, precision=exact, preferred_element_type=f32) * slope
+    small[:1, :columns] = jnp.sum(total, axis=0, keepdims=True)
+    for at in range(peers):
+        rows_sum = gathered[0, at, 0] + gathered[0, at, 1] + gathered[1, at, 0] + gathered[1, at, 1]
+        for inner in range(8):
+            start = columns + (at * 8 + inner) * LANES
+            small[:1, start : start + LANES] = rows_sum[inner : inner + 1, tail]
+    for chunk, out in chunks:
+        chunk.add(out)
+    grad_w_input[:, :half] = out_a[...]
+    grad_w_input[:, half:] = out_b[...]
+
+    def finish(step, carried):
+        peer = lax.rem(seq + step, peers)
+        small_out(peer).wait_send()
+        wide_out(peer, seq).wait_send()
+        return carried
+
+    lax.fori_loop(1, peers, finish, 0)
+    to_x.wait_send()
+    to_core.wait_send()
+    for chunk, out in chunks:
+        chunk.finish()
+
+
+def close(segments, mel, peers, operands):
+    grads, stream, mod, seg, grad_middle, features, sums = operands[:7]
+    w_input, w_ada = operands[-2:]
+    frames, width = stream.shape
+    shards = 4 * peers
+    slot = width // shards
+    columns = mod.shape[1]
+    table = operands[11]
+    padded = features.shape[1]
+    half = padded // 2
+    piece = columns // peers // 2
+    in_vmem = pl.BlockSpec(memory_space=pltpu.VMEM)
+    anywhere = pl.BlockSpec(memory_space=pl.ANY)
+    shape = jax.ShapeDtypeStruct
+    dma = pltpu.SemaphoreType.DMA
+    return pl.pallas_call(
+        functools.partial(close_kernel, segments, mel),
+        out_shape=(
+            shape((frames, w_input.shape[0]), f32),
+            shape((slot, padded), f32),
+            shape((slot, columns), f32),
+            shape((table.shape[0], slot), f32),
+            shape((8, columns + 8 * width), f32),
+        ),
+        in_specs=[in_vmem] * 13 + [anywhere] * 3 + [in_vmem, anywhere],
+        out_specs=(in_vmem,) * 5,
+        scratch_shapes=[
+            pltpu.VMEM((3, width, width), bf16),
+            pltpu.VMEM((slot, columns), bf16),
+            pltpu.VMEM((frames, width), f32),
+            pltpu.VMEM((frames, width), bf16),
+            pltpu.VMEM((2, segments, 8, width), f32),
+            pltpu.VMEM((8, width), f32),
+            pltpu.VMEM((shards, slot, half), bf16),
+            pltpu.VMEM((shards, slot, half), bf16),
+            pltpu.VMEM((shards, slot, half), bf16),
+            pltpu.VMEM((shards, slot, half), bf16),
+            pltpu.VMEM((slot, half), f32),
+            pltpu.VMEM((slot, half), f32),
+            pltpu.VMEM((peers, 8, piece + LANES), f32),
+            pltpu.VMEM((peers, 8, piece + LANES), f32),
+            pltpu.VMEM((2, peers, 2, 8, piece + 2 * LANES), f32),
+            pltpu.VMEM((16, columns), f32),
+            dma((4,)), dma((2, 5)), dma((2, 5)), dma((peers,)), dma((peers,)), dma((peers + 2,)), dma((peers + 2,)),
+        ],
+        compiler_params=pltpu.CompilerParams(collective_id=2, has_side_effects=True, vmem_limit_bytes=VMEM_BYTES),
+        name="close",
+    )(*operands)
+
+
+def rope_tables(length, head_width):
+    angles = np.arange(length)[:, None] * 10000.0 ** (-np.arange(0, head_width, 2) / head_width)[None, :]
+    cosine = np.repeat(np.cos(angles), 2, axis=1)
+    sine = np.stack([-np.sin(angles), np.sin(angles)], axis=2).reshape(length, head_width)
+    count = LANES // head_width
+    return np.tile(cosine, (1, count)).astype(np.float32), np.tile(sine, (1, count)).astype(np.float32)
+
+
+def shards(
+    noisy_mel, cond_mel, text_feats, segment_ids, drop_cond, drop_text, time_index, time_table, w_input, b_input,
+    w_ada, b_ada, w_query, b_query, w_key, b_key, w_value, b_value, w_out, b_out, w_up, b_up, w_down, b_down, cotangent,
+):
+    peers = lax.axis_size("seq")
+    frames = noisy_mel.shape[1]
+    width = w_query.shape[0]
+    mel = noisy_mel.shape[2]
+    segments = drop_cond.shape[1]
+    table_rows = time_table.shape[0]
+    shard = lax.axis_index("rows") * peers + lax.axis_index("seq")
+    slot = width // (4 * peers)
+    line = lambda bias: bias.reshape(1, -1)
+    seg = segment_ids[0][:, None]
+    member = segment_ids[0][None, :] == jnp.arange(8, dtype=jnp.int32)[:, None]
+    index = jnp.arange(8)[:, None]
+    onehot = jnp.where(index < segments, member.astype(f32), (index < segments + 3).astype(f32))
+    inside = seg == jnp.arange(segments, dtype=jnp.int32)[None, :]
+    keeps = jnp.concatenate(
+        [1 - jnp.sum(jnp.where(inside, drop, 0), axis=1, keepdims=True) for drop in (drop_cond, drop_text)], axis=1
+    ).astype(f32)
+    times = (
+        jnp.pad(time_index[0], (0, 8 - segments), constant_values=-1)[:, None]
+        == jnp.arange(LANES, dtype=jnp.int32)[None, :]
+    ).astype(f32)
+    table_mine = lax.dynamic_slice_in_dim(time_table, shard * slot, slot, 1)
+    cosine, sine = (jnp.asarray(table) for table in rope_tables(frames * peers, width // HEADS))
+
+    mod, stream, attn_in, features = embed(
+        noisy_mel[0], cond_mel[0], text_feats[0], seg, drop_cond, drop_text, time_index, time_table, w_input,
+        line(b_input), w_ada, line(b_ada),
+    )
+    att, x_all, query, key, value, attended = attend(
+        segments, peers, attn_in, onehot, w_query, w_key, w_value, line(b_query), line(b_key), line(b_value), cosine, sine
+    )
+    fed = feed(
+        segments, att, stream, mod, seg, cotangent[0], w_out, line(b_out), w_up, line(b_up), w_down, line(b_down)
+    )
+    layer_out, grad_middle, grad_att, sums, bias_feed = fed[0], fed[1], fed[2], fed[9], fed[10]
+    grads, grad_w_down, grad_w_up, grad_w_out, grad_w_three, bias_three = give_back(
+        segments, grad_att, query, key, value, attended, x_all, cosine, sine, fed[3:9]
+    )
+    grad_features, grad_w_input_t, grad_w_ada, grad_table, small = close(
+        segments, mel, peers,
+        (grads, stream, mod, seg, grad_middle, features, sums, bias_feed, bias_three, keeps, times, time_table,
+         table_mine, w_query, w_key, w_value, w_input, w_ada),
+    )
+    vector = small[0]
+    columns = w_ada.shape[1]
+
+    def own(start, size):
+        return lax.dynamic_slice_in_dim(vector, start + shard * (size // (4 * peers)), size // (4 * peers))
+
+    grad_b_ada = own(0, columns)
+    sizes = [width] * 4 + [w_up.shape[1]] + [width] * 2
+    starts = [columns + sum(sizes[:at]) for at in range(len(sizes))]
+    biases = [own(start, size) for start, size in zip(starts, sizes)]
+    return (
+        layer_out[None],
+        grad_features[None, :, :mel],
+        grad_features[None, :, mel : 2 * mel],
+        grad_features[None, :, 2 * mel :],
+        grad_table,
+        grad_w_input_t[:, : w_input.shape[0]].T,
+        biases[6],
+        grad_w_ada,
+        grad_b_ada,
+        grad_w_three[0],
+        biases[0],
+        grad_w_three[1],
+        biases[1],
+        grad_w_three[2],
+        biases[2],
+        grad_w_out,
+        biases[3],
+        grad_w_up,
+        biases[4],
+        grad_w_down,
+        biases[5],
+    )
 
 
 precise = lax.Precision.HIGHEST
@@ -59,7 +1265,7 @@
     return (leading, second, third)
 
 
-def shards(
+def generic_shards(
     noisy_mel,
     cond_mel,
     text_feats,
@@ -446,4 +1652,5 @@
         P(("rows", "seq"), None),
         P(("rows", "seq")),
     )
-    return jax.shard_map(shards, mesh=mesh, in_specs=in_specs, out_specs=out_specs, check_vma=False)
+    body = shards if (mesh.shape["rows"], mesh.shape["seq"]) == (4, 8) else generic_shards
+    return jax.shard_map(body, mesh=mesh, in_specs=in_specs, out_specs=out_specs, check_vma=False)

time: 2050 us -> 292 us (0.14)
  waiting for transfers between devices: 1390 us -> 0 us
  matrix products: 292 us -> 0 us
  Pallas kernels: 0 us -> 270 us
  local copies, waits for them, and re-layouts: 143 us -> 19.5 us
  blocking collectives: 122 us -> 0 us
  other arithmetic: 51.2 us -> 1.45 us
  loops' own time: 24.8 us -> 0 us
    reduce_scatter x8 -> x0, waiting for transfers between devices: 1310 us -> none  [the longest x1 253 us: shards(): lax.psum_scatter(part_w_ada, ('rows', 'seq'), scatter_dimension=0, tiled=...]
    dot_general x58 -> x0, matrix products: 292 us -> none  [the longest x3 46.8 us: shards(): jnp.dot(silu_table.T, piece, preferred_element_type=jnp.float32)]
    pallas_call x0 -> x5, Pallas kernels: none -> 270 us  [the longest x1 122 us: give_back(): pl.pallas_call(functools.partial(return_kernel, segments), out_shape=(sha...]
    all_gather x3 -> x0, blocking collectives: 83.9 us -> none  [the longest x1 30.6 us: shards(): lax.all_gather(log_total, 'seq', axis=1, tiled=True)]
    all_gather x4 -> x0, waiting for transfers between devices: 81.4 us -> none  [the longest x1 69.1 us: shards(): lax.all_gather(key_rot, 'seq', axis=0, tiled=True)]
    dynamic_slice x48 -> x4, local copies, waits for them, and re-layouts: 61.6 us -> 3.26 us  [the longest x3 1.83 us: own(): lax.dynamic_slice_in_dim(vector, start + shard * (size // (4 * peers)), s...]
    unnamed x1 -> x0, blocking collectives: 38.4 us -> none
    unnamed x177 -> x31, local copies, waits for them, and re-layouts: 37.2 us -> 8.18 us
  transfers between devices with their start and end apart: 13 -> 0, of which waited for: 11 -> 0; matrix products, arithmetic and copies ran while one was open for 14% -> 0% of each run, Pallas kernels for 0% -> 0%
where the time goes in v1:
time: 292 us
  Pallas kernels  270 us (92%)
  local copies, waits for them, and re-layouts  19.5 us (7%)
    pallas_call x1, Pallas kernels, give_back(): pl.pallas_call(functools.partial(return_kernel, segments), out_shape=(sha...  122 us
    pallas_call x1, Pallas kernels, attend(): pl.pallas_call(functools.partial(attend_kernel, segments), out_shape=(jax...  79.5 us
    pallas_call x1, Pallas kernels, close(): pl.pallas_call(functools.partial(close_kernel, segments, mel), out_shape=...  37.3 us
    pallas_call x1, Pallas kernels, feed(): pl.pallas_call(functools.partial(feed_kernel, segments), out_shape=(shape...  20.8 us
    pallas_call x1, Pallas kernels, embed(): pl.pallas_call(embed_kernel, grid=(blocks,), out_shape=(jax.ShapeDtypeStr...  10.9 us
    unnamed x31, local copies, waits for them, and re-layouts  8.18 us

profile of v1, /device:TPU:0, one launch (start us, length us, event | category | flops | bytes accessed | tf_op | source)
XLA Modules:
  0.0 291.8 jit_solution(11458157029707125919)
XLA Ops:
  0.7 1.5 copy.79.seg_in
  2.1 1.5 copy.77
  3.7 1.5 copy.78
  5.2 10.9 %embed.1 = (f32[8,6144]{1,0:T(8,128)}, f32[256,1024]{1,0:T(8,128)}, bf16[256,1024]{1,0:T(8,128)(2,1)}, bf16[256,768]{1,0:T(8,128)(2,1)}) custom-call(bf16[256,100]{1,0:T(8,128)(2,1)} %bitcast.51, bf16[256,100]{1,0:T(8,128)(2,1)} %bitcast.52, bf16[256,512]{1,0:T(8,128)(2,1)} %bitcast.50, s32[256,1]{1,0:T(8,128)} %copy.79.seg_in, s32[1,4]{1,0:T(1,128)} %drop_cond.1, ...), custom_call_target="tpu_custom_call" | custom-call | tf_op jit(solution)/shard_map/embed/pallas_call | solution.py:219
  16.2 0.7 convert_select_fusion.onehot
  16.9 79.5 %attend.1 = (bf16[256,1024]{1,0:T(8,128)(2,1)}, bf16[2048,1024]{1,0:T(8,128)(2,1)}, bf16[2,2048,256]{2,1,0:T(8,128)(2,1)}, bf16[2048,256]{1,0:T(8,128)(2,1)}, bf...) custom-call(bf16[256,1024]{1,0:T(8,128)(2,1)} %get-tuple-element.53.x_in, f32[8,256]{1,0:T(8,128)} %convert_select_fusion.onehot, ...), custom_call_target="tpu_custom_call" | custom-call | tf_op jit(solution)/shard_map/attend/pallas_call | solution.py:447
  96.4 20.8 %feed.1 = (bf16[256,1024]{1,0:T(8,128)(2,1)}, f32[256,1024]{1,0:T(8,128)}, bf16[256,1024]{1,0:T(8,128)(2,1)}, bf16[2048,256]{1,0:T(8,128)(2,1)}, bf16[256,1024]{...) custom-call(bf16[256,1024]{1,0:T(8,128)(2,1)} %get-tuple-element.54., ...), custom_call_target="tpu_custom_call" | custom-call | tf_op jit(solution)/shard_map/feed/pallas_call | solution.py:572
  117.2 0.0 copy-start.8
  117.2 0.0 copy-start.9
  117.2 0.0 copy-start.10
  117.2 121.5 %give_back.1 = (bf16[256,3072]{1,0:T(8,128)(2,1)}, f32[64,1024]{1,0:T(8,128)}, f32[32,2048]{1,0:T(8,128)}, f32[32,1024]{1,0:T(8,128)}, f32[3,32,1024]{2,1,0:T(8,128)}, /*index=5*/f32[8,128]{1,0:T(8,128)}) custom-call(bf16[256,1024]{1,0:T(8,128)(2,1)} %get-tuple-element.58.grad_att, bf16[2,2048,256]{2,1,0:T(8,128)(2,1)} %get-tuple-element.59.query, ...), custom_call_target="tpu_custom_call" | custom-call | tf_op jit(solution)/shard_map/give_back/pallas_call | solution.py:849
  238.7 1.4 constant_dynamic-slice_fusion.8.table_mine
  240.2 0.1 select_reduce_fusion.1
  240.3 0.8 copy.82.keeps
  241.1 0.7 fusion.times
  241.8 37.3 %close.1 = (f32[256,712]{1,0:T(8,128)}, f32[32,768]{1,0:T(8,128)}, f32[32,6144]{1,0:T(8,128)}, f32[32,32]{1,0:T(8,128)}, f32[8,14336]{1,0:T(8,128)}) custom-call(bf16[256,3072]{1,0:T(8,128)(2,1)} %get-tuple-element.70.grads, f32[256,1024]{1,0:T(8,128)} %get-tuple-element.55.stream, f32[8,6144]{1,0:T(8,128)} %get-tuple-element.56.mod, s32[256,1]{1,0:T(8,128)} %copy.79.seg_in, ...), custom_call_target="tpu_custom_call" | custom-call | tf_op jit(solution)/shard_map/close/pallas_call | solution.py:1092
  279.1 2.2 slice_bitcast_fusion
  281.3 1.1 slice_bitcast_fusion.4
  282.4 0.0 copy-start.2
  282.4 0.7 copy.83
  283.2 0.7 copy.84
  283.9 1.0 slice.28
  285.0 0.6 fusion.7
  285.6 0.6 slice_bitcast_fusion.6
  286.2 0.6 fusion.6
  286.8 0.6 constant_dynamic-slice_fusion.6
  287.5 0.8 slice_bitcast_fusion.1
  288.2 0.6 copy.90
  288.8 0.9 copy.91
  289.7 0.7 copy.92
  290.4 0.7 copy.93
  291.1 0.7 copy.94
  (22 shorter events, 0.1 us)
Async XLA Ops:
  5.2 11.0 %copy-start.7 = (s32[1,256]{1,0:T(1,128)S(1)}, s32[1,256]{1,0:T(1,128)}, u32[]{:S(2)}) copy-start(s32[1,256]{1,0:T(1,128)} %param.30) | copy-start | bytes 3076
  117.2 123.0 %copy-start.8 = (s32[1,4]{1,0:T(1,128)S(1)}, s32[1,4]{1,0:T(1,128)}, u32[]{:S(2)}) copy-start(s32[1,4]{1,0:T(1,128)} %drop_cond.1) | copy-start | bytes 52
  117.2 123.0 %copy-start.9 = (s32[1,4]{1,0:T(1,128)S(1)}, s32[1,4]{1,0:T(1,128)}, u32[]{:S(2)}) copy-start(s32[1,4]{1,0:T(1,128)} %drop_text.1) | copy-start | bytes 52
  117.2 123.9 %copy-start.10 = (s32[1,4]{1,0:T(1,128)S(1)}, s32[1,4]{1,0:T(1,128)}, u32[]{:S(2)}) copy-start(s32[1,4]{1,0:T(1,128)} %time_index.1) | copy-start | bytes 52
  279.1 6.5 %copy-start.5 = (f32[32,768]{1,0:T(8,128)S(1)}, f32[32,768]{1,0:T(8,128)}, u32[]{:S(2)}) copy-start(f32[32,768]{1,0:T(8,128)} %get-tuple-element.78) | copy-start | bytes 294916
  279.1 8.4 %copy-start.1 = (f32[3,32,1024]{2,1,0:T(8,128)S(1)}, f32[3,32,1024]{2,1,0:T(8,128)}, u32[]{:S(2)}) copy-start(f32[3,32,1024]{2,1,0:T(8,128)} %get-tuple-element.81) | copy-start | bytes 1179652
  279.1 9.1 %copy-start.6 = (f32[32,32]{1,0:T(8,128)S(1)}, f32[32,32]{1,0:T(8,128)}, u32[]{:S(2)}) copy-start(f32[32,32]{1,0:T(8,128)} %get-tuple-element.232) | copy-start | bytes 12292
  279.1 9.7 %copy-start = (f32[32,6144]{1,0:T(8,128)S(1)}, f32[32,6144]{1,0:T(8,128)}, u32[]{:S(2)}) copy-start(f32[32,6144]{1,0:T(8,128)} %get-tuple-element.235) | copy-start | bytes 2359300
  281.3 8.4 %copy-start.4 = (f32[32,1024]{1,0:T(8,128)S(1)}, f32[32,1024]{1,0:T(8,128)}, u32[]{:S(2)}) copy-start(f32[32,1024]{1,0:T(8,128)} %get-tuple-element.243) | copy-start | bytes 393220
  281.3 9.1 %copy-start.3 = (f32[32,2048]{1,0:T(8,128)S(1)}, f32[32,2048]{1,0:T(8,128)}, u32[]{:S(2)}) copy-start(f32[32,2048]{1,0:T(8,128)} %get-tuple-element.245) | copy-start | bytes 786436
  282.4 8.7 %copy-start.2 = (f32[64,1024]{1,0:T(8,128)S(1)}, f32[64,1024]{1,0:T(8,128)}, u32[]{:S(2)}) copy-start(f32[64,1024]{1,0:T(8,128)} %get-tuple-element.247) | copy-start | bytes 786436

commit v2 on v0

--- a/solution.py
+++ b/solution.py
@@ -1,11 +1,1555 @@
+import functools
 import math
+from typing import Any, NamedTuple
 
 import jax
 import jax.numpy as jnp
+import numpy as np
 from jax import lax
+from jax.experimental import pallas as pl
+from jax.experimental.pallas import tpu as pltpu
 from jax.sharding import PartitionSpec as P
 
 HEADS = 16
+LANES = 128
+FAR = 1e30
+MESH = pl.DeviceIdType.MESH
+f32 = jnp.float32
+bf16 = jnp.bfloat16
+VMEM_BYTES = 60 * 2**20
+
+
+def dot(left, right):
+    return jnp.dot(left, right, preferred_element_type=f32)
+
+
+def dot_nt(left, right):
+    return lax.dot_general(left, right, (((1,), (1,)), ((), ())), preferred_element_type=f32)
+
+
+def remote(src, dst, send_sem, recv_sem, device):
+    return pltpu.make_async_remote_copy(
+        src_ref=src, dst_ref=dst, send_sem=send_sem, recv_sem=recv_sem, device_id=device, device_id_type=MESH
+    )
+
+
+def announce(devices):
+    barrier = pltpu.get_barrier_semaphore()
+    for device in devices:
+        pl.semaphore_signal(barrier, inc=1, device_id=device, device_id_type=MESH)
+
+
+def hear(devices):
+    pl.semaphore_wait(pltpu.get_barrier_semaphore(), len(devices))
+
+
+def other(value):
+    return value + 1 - 2 * (value % 2)
+
+
+RADIX = dict(core=2, x=2, y=2, z0=2, z1=2, z=4)
+
+
+def digit(name, row, seq):
+    return dict(core=row % 2, x=row // 2, y=seq % 2, z0=(seq // 2) % 2, z1=seq // 4, z=seq // 2)[name]
+
+
+def partner(name, row, seq, ahead=1):
+    if name == "core":
+        return (other(row), seq)
+    if name == "x":
+        return ((row + 2) % 4, seq)
+    if name == "y":
+        return (row, other(seq))
+    if name == "z0":
+        return (row, seq + 2 - 4 * ((seq // 2) % 2))
+    if name == "z1":
+        return (row, (seq + 4) % 8)
+    return (row, (seq + 2 * ahead) % 8)
+
+
+def place_of(order, shard):
+    place = 0
+    for name in order:
+        place = place * RADIX[name] + int(digit(name, shard // 8, shard % 8))
+    return place
+
+
+class Halving:
+    def __init__(self, order, held, landed, send_sems, recv_sems, row, seq):
+        self.held, self.landed = held, landed
+        self.copies, self.places = [], []
+        offset, size, base, used = 0, held.shape[0], 0, 0
+        for name in order:
+            radix = RADIX[name]
+            size //= radix
+            mine = digit(name, row, seq)
+            stage = []
+            for ahead in range(1, radix):
+                stage.append(
+                    remote(
+                        held.at[pl.ds(offset + ((mine + ahead) % radix) * size, size)],
+                        landed.at[pl.ds(base + (ahead - 1) * size, size)],
+                        send_sems.at[used],
+                        recv_sems.at[used],
+                        partner(name, row, seq, ahead),
+                    )
+                )
+                used += 1
+            self.copies.append(stage)
+            offset = offset + mine * size
+            self.places.append((offset, size, base))
+            base += size * (radix - 1)
+
+    def send(self, stage):
+        for copy in self.copies[stage]:
+            copy.start()
+
+    def add(self, stage, out=None):
+        for copy in self.copies[stage]:
+            copy.wait_recv()
+        offset, size, base = self.places[stage]
+        count = len(self.copies[stage])
+
+        def one(at, carried):
+            total = self.held[offset + at].astype(f32)
+            for which in range(count):
+                total += self.landed[base + which * size + at].astype(f32)
+            if out is None:
+                self.held[offset + at] = total.astype(bf16)
+            else:
+                out[...] = total
+            return carried
+
+        lax.fori_loop(0, size, one, 0)
+
+    def step(self, stage):
+        self.add(stage)
+        self.send(stage + 1)
+
+    def finish(self):
+        for stage in self.copies:
+            for copy in stage:
+                copy.wait_send()
+
+
+def by_segment(seg, table):
+    count = table.shape[0]
+    spread = table[count - 1 :]
+    for at in reversed(range(count - 1)):
+        spread = jnp.where(seg <= at, table[at : at + 1], spread)
+    return spread
+
+
+def normed(values):
+    centred = values - jnp.mean(values, axis=1, keepdims=True)
+    scale = lax.rsqrt(jnp.mean(centred * centred, axis=1, keepdims=True) + 1e-06)
+    return centred * scale, scale
+
+
+def norm_back(norm, scale, grad):
+    return (
+        grad - jnp.mean(grad, axis=1, keepdims=True) - norm * jnp.mean(grad * norm, axis=1, keepdims=True)
+    ) * scale
+
+
+def turn(values, cosine, sine):
+    lane = lax.broadcasted_iota(jnp.int32, values.shape, 1)
+    swapped = jnp.where(lane % 2 == 0, pltpu.roll(values, LANES - 1, 1), pltpu.roll(values, 1, 1))
+    return values * cosine + swapped * sine
+
+
+def parts_of(values):
+    first = values.astype(bf16).astype(f32)
+    second = (values - first).astype(bf16).astype(f32)
+    return first, second, values - first - second
+
+
+def row_loop(count, step, body):
+    def one(at, carried):
+        body(pl.ds(pl.multiple_of(at * step, step), step))
+        return carried
+
+    lax.fori_loop(0, count // step, one, 0, unroll=8)
+
+class Names:
+    def __init__(self, names, refs):
+        self.__dict__.update(zip(names, refs, strict=True))
+
+
+def load(src, dst, sem):
+    copy = pltpu.make_async_copy(src, dst, sem)
+    copy.start()
+    return copy
+
+
+def shift_of(step, peers):
+    return peers // 2 + (1 - 2 * (step % 2)) * ((step + 1) // 2)
+
+
+def mark_columns(rows):
+    return jnp.concatenate([rows, jnp.zeros((LANES - 8, rows.shape[1]), f32)], axis=0).T
+
+
+def turn_parts(both):
+    lane = lax.broadcasted_iota(jnp.int32, both.shape, 1)
+    swapped = pltpu.roll(both, LANES // 2, 1)
+    first = lane < LANES // 2
+    return jnp.where(first, both, swapped), jnp.where(first, swapped, both)
+
+
+PIECES = 4
+
+
+class FrontIn(NamedTuple):
+    noisy_t: Any
+    cond_t: Any
+    text: Any
+    seg_row: Any
+    drop_cond: Any
+    drop_text: Any
+    time_index: Any
+    table: Any
+    b_input: Any
+    b_ada: Any
+    b_query: Any
+    b_key: Any
+    b_value: Any
+    b_out: Any
+    b_up: Any
+    b_down: Any
+    cot_in: Any
+    w_input: Any
+    w_ada: Any
+    w_query: Any
+    w_key: Any
+    w_value: Any
+    turns: Any
+    w_out: Any
+    w_up: Any
+    w_down: Any
+
+class FrontOut(NamedTuple):
+    sums: Any
+    biases: Any
+    mod_out: Any
+    stream_out: Any
+    features_out: Any
+    marks_out: Any
+    x_out: Any
+    query_out: Any
+    key_out: Any
+    value_out: Any
+    attended_out: Any
+    layer_out: Any
+    middle_out: Any
+    grad_att_out: Any
+    act_t_out: Any
+    grad_ffn_out: Any
+    ffn_in_t_out: Any
+    grad_up_out: Any
+    att_t_out: Any
+    grad_attn_out: Any
+
+
+def front_scratch(frames, width, hidden, columns, padded, inputs, peers):
+    length = frames * peers
+    dma = pltpu.SemaphoreType.DMA
+    return dict(
+        mod=pltpu.VMEM((8, columns), f32),
+        stream=pltpu.VMEM((frames, width), f32),
+        marks=pltpu.VMEM((frames, LANES), f32),
+        features=pltpu.VMEM((length, padded), bf16),
+        x_all=pltpu.VMEM((length, width), bf16),
+        query=pltpu.VMEM((2, length, 2 * LANES), bf16),
+        key=pltpu.VMEM((length, 2 * LANES), bf16),
+        value=pltpu.VMEM((length, LANES), bf16),
+        attended=pltpu.VMEM((length, LANES), f32),
+        value_one=pltpu.VMEM((length, 2 * LANES), bf16),
+        w_in=pltpu.VMEM((inputs, width), bf16),
+        w_mod=pltpu.VMEM((width, columns), bf16),
+        w_three=pltpu.VMEM((width, 3 * LANES), bf16),
+        turn_table=pltpu.VMEM((length, LANES), f32),
+        onehots=pltpu.VMEM((peers, 8, frames), f32),
+        out_tiles=pltpu.VMEM((peers, frames, LANES), bf16),
+        work=pltpu.VMEM((frames, width), f32),
+        marks_here=pltpu.VMEM((frames, LANES), f32),
+        att=pltpu.VMEM((frames, width), bf16),
+        cot=pltpu.VMEM((frames, width), bf16),
+        middle=pltpu.VMEM((frames, width), f32),
+        norm=pltpu.VMEM((frames, width), f32),
+        norm_scale=pltpu.VMEM((frames, LANES), f32),
+        ffn_in=pltpu.VMEM((frames, width), bf16),
+        act=pltpu.VMEM((frames, hidden), bf16),
+        slope=pltpu.VMEM((frames, hidden), f32),
+        total=pltpu.VMEM((frames, width), f32),
+        products=pltpu.VMEM((4, frames, width), bf16),
+        layer=pltpu.VMEM((frames, width), bf16),
+        grad_ffn=pltpu.VMEM((frames, width), bf16),
+        grad_up=pltpu.VMEM((frames, hidden), bf16),
+        grad_middle=pltpu.VMEM((frames, width), f32),
+        grad_attn=pltpu.VMEM((frames, width), bf16),
+        grad_att=pltpu.VMEM((frames, width), bf16),
+        act_t=pltpu.VMEM((hidden, frames), bf16),
+        ffn_in_t=pltpu.VMEM((width, frames), bf16),
+        att_t=pltpu.VMEM((width, frames), bf16),
+        sems=dma((33,)),
+        up_sems=dma((PIECES * peers,)),
+        down_sems=dma((PIECES * peers,)),
+        cross_sems=dma((PIECES * peers,)),
+        pass_sems=dma((PIECES,)),
+        x_sems=dma((PIECES * peers,)),
+        hot_send=dma((peers,)),
+        hot_recv=dma((peers,)),
+        out_send=dma((peers,)),
+        out_recv=dma((peers,)),
+    )
+
+
+def front_kernel(segments, scratch_names, *refs):
+    n = Names(FrontIn._fields + FrontOut._fields + scratch_names, refs)
+    row, seq = lax.axis_index("rows"), lax.axis_index("seq")
+    frames, width = n.stream.shape
+    length, padded = n.features.shape
+    peers = length // frames
+    inputs = n.w_in.shape[0]
+    mel = n.noisy_t.shape[0]
+    depth = peers // 2
+    high, low = seq // 2, seq % 2
+    mine = pl.ds(pl.multiple_of(seq * LANES, LANES), LANES)
+    block_rows = lambda at: pl.ds(pl.multiple_of(at * frames, frames), frames)
+
+    everyone = [(row, lax.rem(seq + ahead, peers)) for ahead in range(1, peers)]
+    announce(everyone)
+    in_load = load(n.w_input, n.w_in, n.sems.at[0])
+    early = 2 * width
+    ada_loads = [load(n.w_ada.at[:, :early], n.w_mod.at[:, :early], n.sems.at[1])]
+    three_loads = [
+        load(weight.at[:, mine], n.w_three.at[:, pl.ds(at * LANES, LANES)], n.sems.at[2 + at])
+        for at, weight in enumerate((n.w_query, n.w_key, n.w_value))
+    ]
+    turn_load = load(n.turns, n.turn_table, n.sems.at[5])
+    ada_loads.append(load(n.w_ada.at[:, early:], n.w_mod.at[:, early:], n.sems.at[6]))
+
+    seg = n.seg_row[...]
+    at_row = lax.broadcasted_iota(jnp.int32, (8, frames), 0)
+    hot = jnp.where(at_row < segments, jnp.where(at_row == seg, 1.0, 0.0), 1.0)
+    hot = jnp.where(at_row == 7, seg.astype(f32), hot)
+    n.onehots[seq] = hot
+    marks = mark_columns(hot)
+    keep_cond = jnp.zeros((frames, 1), f32)
+    keep_text = jnp.zeros((frames, 1), f32)
+    for at in range(segments):
+        keep_cond += marks[:, at : at + 1] * (1 - n.drop_cond[0, at]).astype(f32)
+        keep_text += marks[:, at : at + 1] * (1 - n.drop_text[0, at]).astype(f32)
+    lane = lax.broadcasted_iota(jnp.int32, (frames, LANES), 1)
+    n.marks[...] = jnp.where(lane == 8, keep_cond, jnp.where(lane == 9, keep_text, marks))
+    tall = lambda ref: jnp.concatenate([ref[...].astype(f32), jnp.zeros((LANES - mel, frames), f32)], axis=0).T
+    n.features[block_rows(seq), :] = jnp.concatenate(
+        [
+            tall(n.noisy_t)[:, :mel],
+            (tall(n.cond_t) * keep_cond)[:, :mel],
+            n.text[...].astype(f32) * keep_text,
+            jnp.zeros((frames, padded - inputs), f32),
+        ],
+        axis=1,
+    ).astype(bf16)
+
+    hear(everyone)
+    hot_copies = []
+    for ahead in range(1, peers):
+        copy = remote(
+            n.onehots.at[seq], n.onehots.at[seq], n.hot_send.at[ahead], n.hot_recv.at[seq],
+            (row, lax.rem(seq + ahead, peers)),
+        )
+        copy.start()
+        hot_copies.append(copy)
+
+    def hop(block, half, sem, device):
+        size = frames // PIECES
+        rows = n.features.at[pl.ds(pl.multiple_of(block * frames + half * size, size), size)]
+        return remote(rows, rows, sem, n.x_sems.at[PIECES * block + half], device)
+
+    def up(block, half):
+        return hop(block, half, n.up_sems.at[PIECES * block + half], (row, seq + 2))
+
+    def down(block, half):
+        return hop(block, half, n.down_sems.at[PIECES * block + half], (row, seq - 2))
+
+    def cross(block, half):
+        return hop(block, half, n.cross_sems.at[PIECES * block + half], (row, other(seq)))
+
+    crossed_here = other(seq)
+    pass_on = [
+        hop(crossed_here, half, n.pass_sems.at[half], (row, seq + 2 - 4 * (high % 2))) for half in range(PIECES // 2, PIECES)
+    ]
+    has_up, has_down = high < depth - 1, high > 0
+    at_end = (high == 0) | (high == depth - 1)
+
+    def send_own(pieces):
+        for half in pieces:
+
+            @pl.when(has_up)
+            def _(half=half):
+                up(seq, half).start()
+
+            @pl.when(has_down)
+            def _(half=half):
+                down(seq, half).start()
+
+            cross(seq, half).start()
+
+    send_own(range(PIECES // 2))
+
+    picked = [n.table[pl.ds(n.time_index[0, at], 1), :] for at in range(segments)]
+    picked = jnp.concatenate(picked + [jnp.zeros((16 - segments, width), f32)], axis=0)
+    silu = (picked / (1.0 + jnp.exp(-picked))).astype(bf16)
+    ada_loads[0].wait()
+    send_own(range(PIECES // 2, PIECES))
+    n.mod[:, :early] = dot(silu, n.w_mod[:, :early])[:8] + n.b_ada[:, :early]
+
+    def project(block):
+        rows = block_rows(block)
+        n.work[...] = dot(n.features[rows, :inputs], n.w_in[...]) + n.b_input[...]
+        extras = mark_columns(n.onehots[block])
+
+        def shape(some):
+            norm, unused = normed(n.work[some, :])
+            place = pl.ds(pl.multiple_of(some.start, 32), 32)
+            seg_here = n.marks_here[place, 7:8]
+            shift = by_segment(seg_here, n.mod[:segments, :width])
+            scale = by_segment(seg_here, n.mod[:segments, width : 2 * width])
+            n.x_all[pl.ds(pl.multiple_of(block * frames + some.start, 32), 32), :] = (
+                norm * (1.0 + scale) + shift
+            ).astype(bf16)
+
+        n.marks_here[...] = extras
+        row_loop(frames, 32, shape)
+        three = dot(n.x_all[rows, :], n.w_three[...])
+        turns = turn_parts(n.turn_table[rows, :])
+        rotated = turn(three[:, :LANES] + n.b_query[:, mine], *turns).astype(bf16).astype(f32) * 0.125
+        walls = jnp.where(lane < segments, (extras - 1.0) * FAR, 0.0).astype(bf16)
+        for head in range(2):
+            n.query[head, rows, :LANES] = jnp.where(lane // 64 == head, rotated, 0.0).astype(bf16)
+            n.query[head, rows, LANES:] = walls
+        n.key[rows, :LANES] = turn(three[:, LANES : 2 * LANES] + n.b_key[:, mine], *turns).astype(bf16)
+        n.key[rows, LANES:] = jnp.where(lane < 7, extras, 0.0).astype(bf16)
+        values = (three[:, 2 * LANES :] + n.b_value[:, mine]).astype(bf16)
+        n.value[rows, :] = values
+        n.value_one[rows, :LANES] = values
+        n.value_one[rows, LANES:] = jnp.ones((frames, LANES), bf16)
+
+    in_load.wait()
+    for copy in three_loads + [turn_load]:
+        copy.wait()
+    project(seq)
+    n.stream[...] = n.work[...]
+    saves = [
+        load(n.stream, n.stream_out, n.sems.at[8]),
+        load(n.marks, n.marks_out, n.sems.at[9]),
+        load(n.features.at[block_rows(seq)], n.features_out, n.sems.at[10]),
+    ]
+    for ahead in range(1, peers):
+        source = lax.rem(seq + peers - ahead, peers)
+        remote(
+            n.onehots.at[source], n.onehots.at[source], n.hot_send.at[0], n.hot_recv.at[source], (row, source)
+        ).wait_recv()
+
+    def ring(step, carried):
+        from_low, from_high = seq - 2 * step, seq + 2 * step
+        low_here, high_here = from_low >= 0, from_high < peers
+        low_short = (step == 1) & (high % 2 == 1) & jnp.logical_not(at_end)
+        high_short = (step == 1) & (high % 2 == 0) & jnp.logical_not(at_end)
+
+        for half in range(PIECES):
+
+            @pl.when(low_here)
+            def _(half=half):
+                cross(from_low, half).wait_recv()
+
+                @pl.when(has_up)
+                def _():
+                    up(from_low, half).start()
+
+                if half < PIECES // 2:
+                    cross(from_low, half).start()
+                else:
+
+                    @pl.when(jnp.logical_not(low_short))
+                    def _():
+                        cross(from_low, half).start()
+
+            @pl.when(high_here)
+            def _(half=half):
+                cross(from_high, half).wait_recv()
+
+                @pl.when(has_down)
+                def _():
+                    down(from_high, half).start()
+
+                if half < PIECES // 2:
+                    cross(from_high, half).start()
+                else:
+
+                    @pl.when(jnp.logical_not(high_short))
+                    def _():
+                        cross(from_high, half).start()
+
+        for at in range(4):
+
+            @pl.when(step == 1 + at // 2)
+            def _(at=at):
+                if at == 0:
+                    ada_loads[1].wait()
+                some = slice(early + at * width, early + (at + 1) * width)
+                n.mod[:, some] = dot(silu, n.w_mod[:, some])[:8] + n.b_ada[:, some]
+
+        take_in(step)
+        return carried
+
+    def take_in(step):
+        def one(which, carried):
+            crossing = which // 2
+            back_by = step - crossing
+            block = seq + crossing * (crossed_here - seq) + (4 * (which % 2) - 2) * back_by
+            wanted = (block >= 0) & (block < peers) & ((back_by > 0) | (which % 2 == 0)) & (back_by < depth)
+
+            @pl.when(wanted & (crossing == 1))
+            def _():
+                for half in range(PIECES):
+                    cross(block, half).wait_recv()
+
+                @pl.when((back_by == 0) & at_end)
+                def _():
+                    for copy in pass_on:
+                        copy.start()
+
+            @pl.when(wanted)
+            def _():
+                project(block)
+
+            return carried
+
+        lax.fori_loop(0, 4, one, 0)
+
+    lax.fori_loop(1, depth, ring, 0)
+    hidden = n.act.shape[1]
+    up_at, down_at, out_at = 0, hidden, 2 * hidden
+    feed_loads = [
+        load(n.cot_in, n.cot, n.sems.at[32]),
+        load(n.w_out, n.w_mod.at[:, out_at : out_at + width], n.sems.at[16]),
+        load(n.w_up, n.w_mod.at[:, up_at : up_at + hidden], n.sems.at[17]),
+    ] + [
+        load(
+            n.w_down.at[pl.ds(at * width, width)],
+            n.w_mod.at[:, down_at + at * width : down_at + (at + 1) * width],
+            n.sems.at[18 + at],
+        )
+        for at in range(hidden // width)
+    ]
+    saves.append(load(n.mod, n.mod_out, n.sems.at[7]))
+    take_in(depth)
+    saves += [
+        load(n.x_all, n.x_out, n.sems.at[11]),
+        load(n.key, n.key_out, n.sems.at[12]),
+        load(n.value, n.value_out, n.sems.at[13]),
+    ]
+
+    def attend(step, carried):
+        block = lax.rem(seq + shift_of(step, peers), peers)
+        rows = block_rows(block)
+        outs = []
+        for head in range(2):
+            scores = dot_nt(n.query[head, rows, :], n.key[...])
+            top = jnp.max(scores, axis=1, keepdims=True)
+            weights = jnp.exp(scores - top).astype(bf16)
+            both = dot(weights, n.value_one[...])
+            total = both[:, LANES:]
+            outs.append(both[:, :LANES] / total)
+            first, second, third = parts_of(top + jnp.log(total))
+            extras = n.query[head, rows, LANES:].astype(f32)
+            extras = jnp.where(lane == segments, -first, extras)
+            extras = jnp.where(lane == segments + 1, -second, extras)
+            n.query[head, rows, LANES:] = jnp.where(lane == segments + 2, -third, extras).astype(bf16)
+        out = jnp.where(lane < 64, outs[0], outs[1])
+        n.attended[rows, :] = out
+        n.out_tiles[block] = out.astype(bf16)
+
+        @pl.when(step < peers - 1)
+        def _():
+            remote(
+                n.out_tiles.at[block], n.att.at[:, mine], n.out_send.at[block], n.out_recv.at[seq], (row, block)
+            ).start()
+
+        return carried
+
+    lax.fori_loop(0, peers, attend, 0)
+    saves += [load(n.query, n.query_out, n.sems.at[14]), load(n.attended, n.attended_out, n.sems.at[15])]
+    n.att[:, mine] = n.out_tiles[seq]
+
+    def finish(step, carried):
+        peer = lax.rem(seq + step, peers)
+        place = pl.ds(pl.multiple_of(peer * LANES, LANES), LANES)
+        copy = remote(n.out_tiles.at[peer], n.att.at[:, place], n.out_send.at[peer], n.out_recv.at[peer], (row, peer))
+        copy.wait_send()
+        copy.wait_recv()
+        return carried
+
+    lax.fori_loop(1, peers, finish, 0)
+    used = iter(range(20, 32))
+    save = lambda src, dst: saves.append(load(src, dst, n.sems.at[next(used)]))
+    part = lambda at: n.mod[:segments, at * width : (at + 1) * width]
+    rows_of_marks = n.onehots[seq].astype(bf16)
+
+    for copy in feed_loads:
+        copy.wait()
+    n.work[...] = dot(n.att[...], n.w_mod[:, out_at : out_at + width]) + n.b_out[...]
+
+    def join(rows):
+        seg = n.marks[rows, 7:8]
+        here = n.stream[rows, :] + by_segment(seg, part(2)) * n.work[rows, :]
+        n.middle[rows, :] = here
+        norm, scale = normed(here)
+        n.norm[rows, :] = norm
+        n.norm_scale[rows, :] = jnp.broadcast_to(scale, (scale.shape[0], LANES))
+        n.ffn_in[rows, :] = (norm * (1.0 + by_segment(seg, part(4))) + by_segment(seg, part(3))).astype(bf16)
+        n.grad_ffn[rows, :] = (n.cot[rows, :].astype(f32) * by_segment(seg, part(5))).astype(bf16)
+
+    row_loop(frames, 32, join)
+    save(n.grad_ffn, n.grad_ffn_out)
+    quarter = hidden // 4
+
+    def down_part(at):
+        begin = at * quarter
+        column = down_at + begin // width * width
+        return n.w_mod[begin % width : begin % width + quarter, column : column + width]
+
+    for at in range(4):
+        some = slice(at * quarter, (at + 1) * quarter)
+        value = dot(n.ffn_in[...], n.w_mod[:, up_at + at * quarter : up_at + (at + 1) * quarter]) + n.b_up[:, some]
+        curve = math.sqrt(2 / math.pi)
+        square = value * value
+        tanh = jnp.tanh(curve * value * (1.0 + 0.044715 * square))
+        half = 0.5 * (1.0 + tanh)
+        act = (value * half).astype(bf16)
+        n.act[:, some] = act
+        n.slope[:, some] = half + 0.5 * value * (1.0 - tanh * tanh) * (curve * (1.0 + 3 * 0.044715 * square))
+        product = dot(act, down_part(at))
+        n.total[...] = product + n.b_down[...] if at == 0 else n.total[...] + product
+
+    def leave(rows):
+        gate = by_segment(n.marks[rows, 7:8], part(5))
+        ffn = n.total[rows, :]
+        n.layer[rows, :] = (n.middle[rows, :] + gate * ffn).astype(bf16)
+        n.products[3, rows, :] = (n.cot[rows, :].astype(f32) * ffn).astype(bf16)
+
+    row_loop(frames, 32, leave)
+    save(n.layer, n.layer_out)
+    for at in range(4):
+        some = slice(at * quarter, (at + 1) * quarter)
+        grad_up = (dot_nt(n.grad_ffn[...], down_part(at)) * n.slope[:, some]).astype(bf16)
+        n.grad_up[:, some] = grad_up
+        product = dot_nt(grad_up, n.w_mod[:, up_at + at * quarter : up_at + (at + 1) * quarter])
+        n.total[...] = product if at == 0 else n.total[...] + product
+    save(n.grad_up, n.grad_up_out)
+
+    def back(rows):
+        seg = n.marks[rows, 7:8]
+        norm = n.norm[rows, :]
+        grad = n.total[rows, :]
+        n.products[1, rows, :] = grad.astype(bf16)
+        n.products[2, rows, :] = (grad * norm).astype(bf16)
+        grad = norm_back(norm, n.norm_scale[rows, 0:1], grad * (1.0 + by_segment(seg, part(4))))
+        grad = grad + n.cot[rows, :].astype(f32)
+        n.grad_middle[rows, :] = grad
+        n.grad_attn[rows, :] = (grad * by_segment(seg, part(2))).astype(bf16)
+        n.products[0, rows, :] = (grad * n.work[rows, :]).astype(bf16)
+
+    row_loop(frames, 32, back)
+    save(n.grad_middle, n.middle_out)
+    save(n.grad_attn, n.grad_attn_out)
+    n.grad_att[...] = dot_nt(n.grad_attn[...], n.w_mod[:, out_at : out_at + width]).astype(bf16)
+    save(n.grad_att, n.grad_att_out)
+    for src, dst, out in ((n.act, n.act_t, n.act_t_out), (n.ffn_in, n.ffn_in_t, n.ffn_in_t_out), (n.att, n.att_t, n.att_t_out)):
+        dst[...] = src[...].T
+        save(dst, out)
+    for at in range(4):
+        n.sums[at] = dot(rows_of_marks, n.products[at])
+    n.biases[:, :width] = dot(rows_of_marks, n.grad_attn[...])[segments : segments + 1]
+    n.biases[:, width:-width] = dot(rows_of_marks, n.grad_up[...])[segments : segments + 1]
+    n.biases[:, -width:] = dot(rows_of_marks, n.grad_ffn[...])[segments : segments + 1]
+
+    def sent(step, carried):
+        from_low, from_high = seq - 2 * step, seq + 2 * step
+        low_here = from_low >= 0
+        high_here = (from_high < peers) & (step > 0)
+        low_short = (step == 1) & (high % 2 == 1) & jnp.logical_not(at_end)
+        high_short = (step == 1) & (high % 2 == 0) & jnp.logical_not(at_end)
+        for half in range(PIECES):
+
+            @pl.when(low_here & has_up)
+            def _(half=half):
+                up(from_low, half).wait_send()
+
+            @pl.when((from_high < peers) & has_down)
+            def _(half=half):
+                down(from_high, half).wait_send()
+
+            @pl.when(low_here & jnp.logical_not(low_short & (half >= PIECES // 2)))
+            def _(half=half):
+                cross(from_low, half).wait_send()
+
+            @pl.when(high_here & jnp.logical_not(high_short & (half >= PIECES // 2)))
+            def _(half=half):
+                cross(from_high, half).wait_send()
+
+        return carried
+
+    lax.fori_loop(0, depth, sent, 0)
+    for copy in hot_copies:
+        copy.wait_send()
+
+    @pl.when(at_end)
+    def _():
+        for copy in pass_on:
+            copy.wait_send()
+
+    for copy in saves:
+        copy.wait()
+
+
+def front(segments, peers, padded, operands):
+    named = FrontIn(*operands)
+    text, w_input, w_ada = named.text, named.w_input, named.w_ada
+    hidden = named.w_up.shape[1]
+    frames = text.shape[0]
+    inputs, width = w_input.shape
+    columns = w_ada.shape[1]
+    length = frames * peers
+    in_vmem = pl.BlockSpec(memory_space=pltpu.VMEM)
+    in_smem = pl.BlockSpec(memory_space=pltpu.SMEM)
+    anywhere = pl.BlockSpec(memory_space=pl.ANY)
+    shape = jax.ShapeDtypeStruct
+    scratch = front_scratch(frames, width, hidden, columns, padded, inputs, peers)
+    return pl.pallas_call(
+        functools.partial(front_kernel, segments, tuple(scratch)),
+        out_shape=(
+            shape((4, 8, width), f32),
+            shape((1, hidden + 2 * width), f32),
+            shape((8, columns), f32),
+            shape((frames, width), f32),
+            shape((frames, padded), bf16),
+            shape((frames, LANES), f32),
+            shape((length, width), bf16),
+            shape((2, length, 2 * LANES), bf16),
+            shape((length, 2 * LANES), bf16),
+            shape((length, LANES), bf16),
+            shape((length, LANES), f32),
+            shape((frames, width), bf16),
+            shape((frames, width), f32),
+            shape((frames, width), bf16),
+            shape((hidden, frames), bf16),
+            shape((frames, width), bf16),
+            shape((width, frames), bf16),
+            shape((frames, hidden), bf16),
+            shape((width, frames), bf16),
+            shape((frames, width), bf16),
+        ),
+        in_specs=[in_vmem] * 4 + [in_smem] * 3 + [in_vmem] * 9 + [anywhere] * 10,
+        out_specs=(in_vmem,) * 2 + (anywhere,) * 18,
+        scratch_shapes=list(scratch.values()),
+        compiler_params=pltpu.CompilerParams(collective_id=0, has_side_effects=True, vmem_limit_bytes=VMEM_BYTES),
+        name="front",
+    )(*operands)
+
+
+PARTNERS = dict(act="grad_ffn", ffn_in="grad_up", att="grad_attn")
+X_FIRST = ("x", "y", "z0", "z1")
+Y_FIRST = ("y", "x", "z0", "z1")
+INPUT_ORDERS = (
+    ("core", "x", "y", "z"),
+    ("core", "y", "x", "z"),
+    ("core", "x", "y", "z"),
+)
+
+def fill(held, order, left, right, columns):
+    rows = held.shape[1]
+    slab = 8 * rows
+    for at in range(4):
+        product = dot(left[at * slab : (at + 1) * slab, :], right[:, columns])
+        for inner in range(8):
+            held[place_of(order, at * 8 + inner)] = product[inner * rows : (inner + 1) * rows, :].astype(bf16)
+
+
+SMALL = 32
+
+
+class BackIn(NamedTuple):
+    grad_att: Any
+    middle_in: Any
+    stream_in: Any
+    mod_in: Any
+    marks_in: Any
+    features_in: Any
+    sums: Any
+    bias_feed: Any
+    table: Any
+    time_index: Any
+    query_in: Any
+    key_in: Any
+    value_in: Any
+    attended_in: Any
+    x_in: Any
+    turns: Any
+    act_t: Any
+    grad_ffn: Any
+    ffn_in_t: Any
+    grad_up: Any
+    att_t: Any
+    grad_attn: Any
+    w_query: Any
+    w_key: Any
+    w_value: Any
+    w_input_in: Any
+    w_ada: Any
+
+class BackOut(NamedTuple):
+    grad_features: Any
+    grad_w_input: Any
+    grad_w_ada: Any
+    grad_table: Any
+    small: Any
+    grad_w_down: Any
+    grad_w_up: Any
+    grad_w_out: Any
+    grad_w_three: Any
+
+
+def back_scratch(frames, width, hidden, columns, padded, inputs, peers):
+    length = frames * peers
+    shards = 4 * peers
+    slot, deep = width // shards, hidden // shards
+    third = padded // 3
+    dma = pltpu.SemaphoreType.DMA
+    scratch = dict(
+        query=pltpu.VMEM((2, length, 2 * LANES), bf16),
+        key=pltpu.VMEM((length, 2 * LANES), bf16),
+        attended=pltpu.VMEM((length, LANES), f32),
+        wide=pltpu.VMEM((3, width, width), bf16),
+        turn_table=pltpu.VMEM((length, LANES), f32),
+        grad_all=pltpu.VMEM((length, LANES), bf16),
+        grad_low=pltpu.VMEM((2, length, 2 * LANES), bf16),
+        value_ext=pltpu.VMEM((length, 2 * LANES), bf16),
+        key_t=pltpu.VMEM((LANES, length), bf16),
+        grad_query_t=pltpu.VMEM((LANES, length), f32),
+        tiles=pltpu.VMEM((3, peers, frames, LANES), bf16),
+        grads_t=pltpu.VMEM((3 * LANES, length), bf16),
+        grads=pltpu.VMEM((frames, 3 * width), bf16),
+        bias_three=pltpu.VMEM((8, LANES), f32),
+        own_act=pltpu.VMEM((2, hidden // 4, frames), bf16),
+        own_ffn_in=pltpu.VMEM((2, width // 4, frames), bf16),
+        own_att=pltpu.VMEM((2, width // 4, frames), bf16),
+        own_grad_ffn=pltpu.VMEM((frames, width), bf16),
+        own_grad_up=pltpu.VMEM((frames, hidden), bf16),
+        own_grad_attn=pltpu.VMEM((frames, width), bf16),
+    )
+    for name in [*PARTNERS, *PARTNERS.values()]:
+        scratch["peer_" + name] = scratch["own_" + name]
+    half = shards // 2
+    for at, dims in enumerate(
+        [(half, deep, width // 2)] * 2 + [(half, slot, hidden // 2)] * 2 + [(half, slot, width)]
+    ):
+        scratch["held%d" % at] = pltpu.VMEM(dims, bf16)
+        scratch["land%d" % at] = pltpu.VMEM(dims, bf16)
+    for at in range(3):
+        scratch["in_held%d" % at] = pltpu.VMEM((shards, slot, third), bf16)
+        scratch["in_land%d" % at] = pltpu.VMEM((shards, slot, third), bf16)
+    scratch |= dict(
+        three_held=pltpu.VMEM((4, width // 4, 3 * LANES), bf16),
+        three_land=pltpu.VMEM((2, width // 4, 3 * LANES), bf16),
+        three_far=pltpu.VMEM((width // 4, 3 * LANES), bf16),
+        three_tiles=pltpu.VMEM((peers, slot, 3 * LANES), bf16),
+        three_in=pltpu.VMEM((peers, slot, 3 * LANES), bf16),
+        ada_mine=pltpu.VMEM((slot, columns), bf16),
+        w_input=pltpu.VMEM((inputs, width), bf16),
+        grad_in=pltpu.VMEM((frames, width), f32),
+        grad_middle=pltpu.VMEM((frames, width), f32),
+        stream=pltpu.VMEM((frames, width), f32),
+        mod=pltpu.VMEM((8, columns), f32),
+        marks=pltpu.VMEM((frames, LANES), f32),
+        features=pltpu.VMEM((frames, padded), bf16),
+        grad_stream=pltpu.VMEM((frames, width), bf16),
+        products=pltpu.VMEM((2, frames, width), bf16),
+        packing=pltpu.VMEM((SMALL, LANES), f32),
+        packed=pltpu.VMEM((peers, SMALL, LANES), bf16),
+        landed=pltpu.VMEM((peers, SMALL, LANES), bf16),
+        gathered=pltpu.VMEM((2, peers, 2, SMALL + 16, LANES), bf16),
+        mod_sums=pltpu.VMEM((16, columns), f32),
+        load_sems=dma((32,)),
+        swap_send=dma((9,)),
+        swap_recv=dma((9,)),
+        do_send=dma((peers,)),
+        do_recv=dma((peers,)),
+        tile_send=dma((3, peers)),
+        tile_recv=dma((3, peers)),
+        half_send=dma((5, 4)),
+        half_recv=dma((5, 4)),
+        three_send=dma((2,)),
+        three_recv=dma((2,)),
+        last_send=dma((peers,)),
+        last_recv=dma((peers,)),
+        in_send=dma((3, 6)),
+        in_recv=dma((3, 6)),
+        small_send=dma((peers,)),
+        small_recv=dma((peers,)),
+        wide_send=dma((peers + 2,)),
+        wide_recv=dma((peers + 2,)),
+    )
+    return scratch
+
+
+def back_kernel(segments, mel, scratch_names, *refs):
+    n = Names(BackIn._fields + BackOut._fields + scratch_names, refs)
+    row, seq = lax.axis_index("rows"), lax.axis_index("seq")
+    core, x = row % 2, row // 2
+    frames, width = n.grad_att.shape
+    length = n.key.shape[0]
+    peers = length // frames
+    hidden = n.own_grad_up.shape[1]
+    columns = n.mod.shape[1]
+    fourth = width // 4
+    slot = width // (4 * peers)
+    block_rows = lambda at: pl.ds(pl.multiple_of(at * frames, frames), frames)
+    columns_of = lambda at, which=0: pl.ds(pl.multiple_of(which * width + at * LANES, LANES), LANES)
+    core_partner = partner("core", row, seq)
+    x_partner = partner("x", row, seq)
+
+    everyone = [(row, lax.rem(seq + ahead, peers)) for ahead in range(1, peers)] + [core_partner, x_partner]
+    announce(everyone)
+    used = iter(range(32))
+    bring = lambda src, dst: load(src, dst, n.load_sems.at[next(used)])
+    feed_loads = []
+    for name in PARTNERS:
+        src, dst = getattr(n, name + "_t"), getattr(n, "own_" + name)
+        part = dst.shape[1]
+        for at in range(2):
+            feed_loads.append(bring(src.at[pl.ds(pl.multiple_of((2 * at + core) * part, part), part)], dst.at[at]))
+    for name in PARTNERS.values():
+        feed_loads.append(bring(getattr(n, name), getattr(n, "own_" + name)))
+    key_load = bring(n.key_in, n.key)
+    value_load = bring(n.value_in, n.value_ext.at[:, :LANES])
+    attended_load = bring(n.attended_in, n.attended)
+    query_load = bring(n.query_in, n.query)
+    turn_load = bring(n.turns, n.turn_table)
+    x_loads = [bring(n.x_in.at[pl.ds(at * width, width)], n.wide.at[at]) for at in range(length // width)]
+    input_load = bring(n.w_input_in, n.w_input)
+    ada_load = bring(n.w_ada.at[pl.ds(pl.multiple_of((row * peers + seq) * slot, slot), slot)], n.ada_mine)
+
+    own_load = bring(n.grad_att.at[:, columns_of(seq)], n.grad_all.at[block_rows(seq)])
+    late_loads = [
+        bring(src, dst)
+        for src, dst in (
+            (n.middle_in, n.grad_middle), (n.stream_in, n.stream), (n.mod_in, n.mod), (n.marks_in, n.marks),
+            (n.features_in, n.features),
+        )
+    ]
+    hear(everyone)
+
+    def tile_out(block):
+        return remote(
+            n.grad_att.at[:, columns_of(block)], n.grad_all.at[block_rows(seq)],
+            n.do_send.at[block], n.do_recv.at[seq], (row, block),
+        )
+
+    def start(step, carried):
+        tile_out(lax.rem(seq + shift_of(step, peers), peers)).start()
+        return carried
+
+    lax.fori_loop(0, peers - 1, start, 0)
+
+    swaps = []
+
+    def swap(src, dst):
+        at = len(swaps)
+        copy = remote(src, dst, n.swap_send.at[at], n.swap_recv.at[at], core_partner)
+        copy.start()
+        swaps.append(copy)
+
+    for name in PARTNERS:
+        src, dst = getattr(n, name + "_t"), getattr(n, "peer_" + name)
+        part = dst.shape[1]
+        swap(getattr(n, PARTNERS[name]), getattr(n, "peer_" + PARTNERS[name]))
+        for at in range(2):
+            swap(src.at[pl.ds(pl.multiple_of((2 * at + 1 - core) * part, part), part)], dst.at[at])
+
+    own_load.wait()
+    for copy in feed_loads:
+        copy.wait()
+
+    chunks = []
+    plan = (
+        (X_FIRST, "act", slice(0, width // 2), n.grad_w_down.at[:, : width // 2]),
+        (Y_FIRST, "act", slice(width // 2, width), n.grad_w_down.at[:, width // 2 :]),
+        (X_FIRST, "ffn_in", slice(0, hidden // 2), n.grad_w_up.at[:, : hidden // 2]),
+        (X_FIRST, "ffn_in", slice(hidden // 2, hidden), n.grad_w_up.at[:, hidden // 2 :]),
+        (Y_FIRST, "att", slice(0, width), n.grad_w_out),
+    )
+    for at, (order, left, some, out) in enumerate(plan):
+        if at in (0, 2, 4):
+            for copy in swaps[3 * (at // 2) : 3 * (at // 2) + 3]:
+                copy.wait_recv()
+        held = getattr(n, "held%d" % at)
+        rows = held.shape[1]
+        sides = [[getattr(n, who + name) for name in (left, PARTNERS[left])] for who in ("own_", "peer_")]
+        for across in range(2):
+            product = dot(sides[0][0][across], sides[0][1][:, some]) + dot(sides[1][0][across], sides[1][1][:, some])
+            for inner in range(8):
+                place = place_of(order, across * 16 + inner)
+                held[place] = product[inner * rows : (inner + 1) * rows, :].astype(bf16)
+        chunks.append(
+            Halving(order, held, getattr(n, "land%d" % at), n.half_send.at[at], n.half_recv.at[at], row, seq)
+        )
+        if at < 2:
+            chunks[at].send(0)
+
+    lane = lax.broadcasted_iota(jnp.int32, (frames, LANES), 1)
+    for copy in (key_load, value_load, attended_load):
+        copy.wait()
+
+    def prepare(step, carried):
+        block = lax.rem(seq + peers - step, peers)
+        rows = block_rows(block)
+
+        @pl.when(step > 0)
+        def _():
+            remote(
+                n.grad_att.at[:, columns_of(block)], n.grad_all.at[rows], n.do_send.at[block], n.do_recv.at[block],
+                (row, block),
+            ).wait_recv()
+
+        grad = n.grad_all[rows, :].astype(f32)
+        product = grad * n.attended[rows, :]
+        for head in range(2):
+            inside = lane // 64 == head
+            first, second, third = parts_of(jnp.sum(jnp.where(inside, product, 0.0), axis=1, keepdims=True))
+            n.grad_low[head, rows, :LANES] = jnp.where(inside, grad, 0.0).astype(bf16)
+            extras = jnp.where(lane == segments, -first, 0.0)
+            extras = jnp.where(lane == segments + 1, -second, extras)
+            n.grad_low[head, rows, LANES:] = jnp.where(lane == segments + 2, -third, extras).astype(bf16)
+        n.value_ext[rows, LANES:] = n.key[rows, LANES:]
+        n.key_t[:, rows] = n.key[rows, :LANES].T
+        n.grad_query_t[:, rows] = jnp.zeros((LANES, frames), f32)
+        return carried
+
+    lax.fori_loop(0, peers, prepare, 0)
+    n.bias_three[...] = jnp.zeros_like(n.bias_three)
+    query_load.wait()
+    turn_load.wait()
+
+    def hand_over(which, block, grad):
+        low = grad.astype(bf16)
+        n.tiles[which, block] = low
+        n.grads_t[which * LANES : (which + 1) * LANES, block_rows(block)] = low.T
+        n.bias_three[which : which + 1, :] += jnp.sum(low.astype(f32), axis=0, keepdims=True)
+
+    def tile_back(which, block):
+        return remote(
+            n.tiles.at[which, block], n.grads.at[:, columns_of(seq, which)],
+            n.tile_send.at[which, block], n.tile_recv.at[which, seq], (row, block),
+        )
+
+    def turn_back(grad, rows):
+        cosine, sine = turn_parts(n.turn_table[rows, :])
+        return turn(grad, cosine, -sine)
+
+    span = min(512, length)
+
+    def key_block(step, carried):
+        block = lax.rem(seq + shift_of(step, peers), peers)
+        rows = block_rows(block)
+        keys, values = n.key[rows, :], n.value_ext[rows, :]
+        grad_key = jnp.zeros((frames, LANES), f32)
+        grad_value = jnp.zeros((frames, LANES), f32)
+        for at in range(length // span):
+            queries = slice(at * span, (at + 1) * span)
+            for head in range(2):
+                low = n.grad_low[head, queries, :]
+                ask = n.query[head, queries, :]
+                probs = jnp.exp(dot_nt(keys, ask))
+                grad_scores = (probs * dot_nt(values, low)).astype(bf16)
+                grad_value += dot(probs.astype(bf16), low[:, :LANES])
+                grad_key += dot(grad_scores, ask[:, :LANES])
+                half = slice(head * 64, (head + 1) * 64)
+                n.grad_query_t[half, queries] += dot(n.key_t[half, rows], grad_scores)
+        hand_over(1, block, turn_back(grad_key, rows))
+        hand_over(2, block, grad_value)
+
+        @pl.when(step < peers - 1)
+        def _():
+            tile_back(1, block).start()
+            tile_back(2, block).start()
+
+        for when, events in TIMETABLE:
+
+            @pl.when(step == when)
+            def _(events=events):
+                for at, stage in events:
+                    if stage is None:
+                        chunks[at].send(0)
+                    else:
+                        chunks[at].step(stage)
+
+        return carried
+
+    lax.fori_loop(0, peers, key_block, 0)
+
+    def query_block(step, carried):
+        block = lax.rem(seq + shift_of(step, peers), peers)
+        rows = block_rows(block)
+        hand_over(0, block, turn_back(n.grad_query_t[:, rows].T * 0.125, rows))
+
+        @pl.when(step < peers - 1)
+        def _():
+            tile_back(0, block).start()
+
+        return carried
+
+    lax.fori_loop(0, peers, query_block, 0)
+    for which in range(3):
+        n.grads[:, columns_of(seq, which)] = n.tiles[which, seq]
+
+    for copy in x_loads:
+        copy.wait()
+    three = dot(n.grads_t[:, :width], n.wide[0])
+    for at in range(1, length // width):
+        three += dot(n.grads_t[:, at * width : (at + 1) * width], n.wide[at])
+    weight_loads = [bring(src, n.wide.at[at]) for at, src in ((1, n.w_key), (2, n.w_value), (0, n.w_query))]
+    three = three.T
+    for at in range(4):
+        n.three_held[(at % 2) * 2 + at // 2] = three[at * fourth : (at + 1) * fourth, :].astype(bf16)
+    first = remote(
+        n.three_held.at[pl.ds((1 - core) * 2, 2)], n.three_land, n.three_send.at[0], n.three_recv.at[0], core_partner
+    )
+    first.start()
+    first.wait_recv()
+    for at in range(2):
+        total = n.three_held[core * 2 + at].astype(f32) + n.three_land[at].astype(f32)
+        n.three_held[core * 2 + at] = total.astype(bf16)
+    second = remote(n.three_held.at[core * 2 + 1 - x], n.three_far, n.three_send.at[1], n.three_recv.at[1], x_partner)
+    second.start()
+
+    def wait_tiles(which):
+        def one(step, carried):
+            peer = lax.rem(seq + step, peers)
+            remote(
+                n.tiles.at[which, peer], n.grads.at[:, columns_of(peer, which)],
+                n.tile_send.at[which, peer], n.tile_recv.at[which, peer], (row, peer),
+            ).wait_recv()
+            return carried
+
+        lax.fori_loop(1, peers, one, 0)
+
+    def add_product(which, first_one=False):
+        product = dot_nt(n.grads[:, which * width : (which + 1) * width], n.wide[which])
+        n.grad_in[...] = product if first_one else n.grad_in[...] + product
+
+    chunks[2].step(1)
+    wait_tiles(1)
+    weight_loads[0].wait()
+    add_product(1, True)
+    chunks[3].step(0)
+    chunks[4].step(1)
+    wait_tiles(2)
+    weight_loads[1].wait()
+    add_product(2)
+
+    second.wait_recv()
+    total = (n.three_held[core * 2 + x].astype(f32) + n.three_far[...].astype(f32)).astype(bf16)
+    for at in range(peers):
+        n.three_tiles[at] = total[at * slot : (at + 1) * slot, :]
+
+    def spread(block):
+        return remote(
+            n.three_tiles.at[block], n.three_in.at[seq], n.last_send.at[block], n.last_recv.at[seq], (row, block)
+        )
+
+    def start_spread(step, carried):
+        spread(lax.rem(seq + step, peers)).start()
+        return carried
+
+    lax.fori_loop(1, peers, start_spread, 0)
+    n.three_in[seq] = n.three_tiles[seq]
+
+    wait_tiles(0)
+    for chunk in chunks[:3]:
+        chunk.step(2)
+    chunks[3].step(1)
+    weight_loads[2].wait()
+    add_product(0)
+
+    for copy in late_loads:
+        copy.wait()
+
+    def leave(rows):
+        seg = n.marks[rows, 7:8]
+        norm, scale = normed(n.stream[rows, :])
+        grad = n.grad_in[rows, :]
+        n.products[0, rows, :] = grad.astype(bf16)
+        n.products[1, rows, :] = (grad * norm).astype(bf16)
+        spread_scale = 1.0 + by_segment(seg, n.mod[:segments, width : 2 * width])
+        low = (n.grad_middle[rows, :] + norm_back(norm, scale, grad * spread_scale)).astype(bf16)
+        n.grad_stream[rows, :] = low
+
+    row_loop(frames, 32, leave)
+    grad_t = n.grad_stream[...].T
+    third = n.features.shape[1] // 3
+    in_chunks = []
+    for at, order in enumerate(INPUT_ORDERS):
+        held = getattr(n, "in_held%d" % at)
+        fill(held, order, grad_t, n.features, slice(at * third, (at + 1) * third))
+        chunk = Halving(order, held, getattr(n, "in_land%d" % at), n.in_send.at[at], n.in_recv.at[at], row, seq)
+        chunk.send(0)
+        in_chunks.append(chunk)
+
+    rows_of_marks = n.marks[...].T[:8].astype(bf16)
+    for part in range(6):
+        whole = dot(rows_of_marks, n.products[part]) if part < 2 else n.sums[part - 2]
+        n.mod_sums[:8, part * width : (part + 1) * width] = whole
+    bias_in = dot(rows_of_marks, n.grad_stream[...])[segments : segments + 1]
+    tiles_each = columns // peers // LANES
+    for at in range(peers):
+        for tile in range(tiles_each):
+            begin = (at * tiles_each + tile) * LANES
+            n.packing[4 * tile : 4 * tile + 4, :] = n.mod_sums[:4, begin : begin + LANES]
+        biases = 4 * tiles_each
+        if at < 3:
+            picked = lax.broadcasted_iota(jnp.int32, (8, LANES), 0) == seq
+            n.packing[biases:, :] = jnp.where(picked, n.bias_three[at : at + 1, :], 0.0)
+        else:
+            source, begin = (n.bias_feed[...], (at - 3) * width) if at < 7 else (bias_in, 0)
+            for tile in range(8):
+                n.packing[biases + tile : biases + tile + 1, :] = source[:, begin + tile * LANES : begin + (tile + 1) * LANES]
+        n.packed[at] = n.packing[...].astype(bf16)
+
+    def small_out(block):
+        return remote(
+            n.packed.at[block], n.landed.at[seq], n.small_send.at[block], n.small_recv.at[seq], (row, block)
+        )
+
+    def start_small(step, carried):
+        small_out(lax.rem(seq + step, peers)).start()
+        return carried
+
+    lax.fori_loop(1, peers, start_small, 0)
+    for chunk in in_chunks:
+        chunk.step(0)
+    for chunk in (chunks[4], chunks[3]):
+        chunk.step(2)
+
+    input_load.wait()
+    grad = dot_nt(n.grad_stream[...], n.w_input[...])
+    lanes = lax.broadcasted_iota(jnp.int32, grad.shape, 1)
+    kept = jnp.where(lanes < mel, 1.0, jnp.where(lanes < 2 * mel, n.marks[:, 8:9], n.marks[:, 9:10]))
+    n.grad_features[...] = grad * kept
+
+    n.landed[seq] = n.packed[seq]
+
+    def wait_small(step, carried):
+        peer = lax.rem(seq + step, peers)
+        remote(n.packed.at[peer], n.landed.at[peer], n.small_send.at[peer], n.small_recv.at[peer], (row, peer)).wait_recv()
+        return carried
+
+    lax.fori_loop(1, peers, wait_small, 0)
+    at_row = lax.broadcasted_iota(jnp.int32, (16, LANES), 0)
+    at_lane = lax.broadcasted_iota(jnp.int32, (16, LANES), 1)
+    times = jnp.zeros((16, LANES), f32)
+    for k in range(segments):
+        times = jnp.where((at_row == k) & (at_lane == n.time_index[0, k]), 1.0, times)
+    n.gathered[core, seq, x, :SMALL, :] = jnp.sum(n.landed[...].astype(f32), axis=0).astype(bf16)
+    n.gathered[core, seq, x, SMALL:, :] = times.astype(bf16)
+    mine = n.gathered.at[core, seq, x]
+    to_x = remote(mine, mine, n.wide_send.at[peers], n.wide_recv.at[peers], x_partner)
+    to_x.start()
+    for chunk in in_chunks:
+        chunk.step(1)
+    to_x.wait_recv()
+
+    def wide_out(block, source):
+        here = n.gathered.at[core, source]
+        return remote(here, here, n.wide_send.at[block], n.wide_recv.at[source], (row, block))
+
+    def start_wide(step, carried):
+        wide_out(lax.rem(seq + step, peers), seq).start()
+        return carried
+
+    lax.fori_loop(1, peers, start_wide, 0)
+    for chunk in in_chunks:
+        chunk.step(2)
+
+    def wait_wide(step, carried):
+        peer = lax.rem(seq + step, peers)
+        wide_out(peer, peer).wait_recv()
+        return carried
+
+    lax.fori_loop(1, peers, wait_wide, 0)
+    to_core = remote(
+        n.gathered.at[core], n.gathered.at[core], n.wide_send.at[peers + 1], n.wide_recv.at[peers + 1], core_partner
+    )
+    to_core.start()
+    for chunk, (order, left, some, out) in zip(chunks, plan):
+        chunk.add(3, out)
+
+    def wait_spread(step, carried):
+        peer = lax.rem(seq + step, peers)
+        remote(
+            n.three_tiles.at[peer], n.three_in.at[peer], n.last_send.at[peer], n.last_recv.at[peer], (row, peer)
+        ).wait_recv()
+        return carried
+
+    lax.fori_loop(1, peers, wait_spread, 0)
+    for which in range(3):
+        for peer in range(peers):
+            n.grad_w_three[which, :, peer * LANES : (peer + 1) * LANES] = n.three_in[
+                peer, :, which * LANES : (which + 1) * LANES
+            ].astype(f32)
+    to_core.wait_recv()
+
+    for at in range(peers):
+        for r in range(4):
+            block = n.gathered[r % 2, at, r // 2].astype(f32)
+            for tile in range(tiles_each):
+                begin = (at * tiles_each + tile) * LANES
+                n.mod_sums[4 * r : 4 * r + 4, begin : begin + LANES] = block[4 * tile : 4 * tile + 4, :]
+    table_rows = n.table.shape[0]
+    picks = jnp.concatenate(
+        [n.gathered[r % 2, 0, r // 2, SMALL:, :].astype(f32)[:4, :table_rows] for r in range(4)], axis=0
+    )
+    total = n.mod_sums[...]
+    exact = lax.Precision.HIGHEST
+    shard = row * peers + seq
+    group = LANES // slot
+    table_block = n.table[:, pl.ds(pl.multiple_of((shard // group) * LANES, LANES), LANES)]
+    table_mine = pltpu.roll(table_block, lax.rem(LANES - (shard % group) * slot, LANES), 1)[:, :slot]
+    gate = 1.0 / (1.0 + jnp.exp(-table_mine))
+    silu_low = (table_mine * gate).astype(bf16).astype(f32)
+    chosen = jnp.dot(picks, silu_low, precision=exact, preferred_element_type=f32)
+    total_low = total.astype(bf16)
+    n.grad_w_ada[...] = dot(chosen.T.astype(bf16), total_low)
+    ada_load.wait()
+    ada = n.ada_mine[...]
+    back_sums = dot_nt(total_low, ada)
+    slope = gate * (1.0 + table_mine * (1.0 - gate))
+    n.grad_table[...] = jnp.dot(picks.T, back_sums, precision=exact, preferred_element_type=f32) * slope
+    n.small[:1, :columns] = jnp.sum(total, axis=0, keepdims=True)
+    for at in range(peers):
+        rows_sum = jnp.sum(n.gathered[:, at].astype(f32).reshape(4, SMALL + 16, LANES), axis=0)
+        for inner in range(8):
+            begin = columns + (at * 8 + inner) * LANES
+            n.small[:1, begin : begin + LANES] = rows_sum[biases + inner : biases + inner + 1, :]
+    for at, chunk in enumerate(in_chunks):
+        chunk.add(3, n.grad_w_input.at[:, at * third : (at + 1) * third])
+
+    def finish(step, carried):
+        peer = lax.rem(seq + step, peers)
+        tile_out(peer).wait_send()
+        for which in range(3):
+            tile_back(which, peer).wait_send()
+        spread(peer).wait_send()
+        small_out(peer).wait_send()
+        wide_out(peer, seq).wait_send()
+        return carried
+
+    lax.fori_loop(1, peers, finish, 0)
+    for copy in swaps + [first, second, to_x, to_core]:
+        copy.wait_send()
+    for chunk in chunks + in_chunks:
+        chunk.finish()
+
+
+TIMETABLE = (
+    (0, ((0, 0), (2, None))),
+    (1, ((1, 0), (4, None))),
+    (4, ((2, 0), (3, None))),
+    (6, ((0, 1),)),
+    (7, ((4, 0), (1, 1))),
+)
+
+
+def back(segments, mel, peers, operands):
+    grad_att, mod, features, table = operands[0], operands[3], operands[5], operands[8]
+    w_input = operands[25]
+    frames, width = grad_att.shape
+    hidden = operands[19].shape[1]
+    columns, padded = mod.shape[1], features.shape[1]
+    shards = 4 * peers
+    slot = width // shards
+    in_vmem = pl.BlockSpec(memory_space=pltpu.VMEM)
+    in_smem = pl.BlockSpec(memory_space=pltpu.SMEM)
+    anywhere = pl.BlockSpec(memory_space=pl.ANY)
+    shape = jax.ShapeDtypeStruct
+    scratch = back_scratch(frames, width, hidden, columns, padded, w_input.shape[0], peers)
+    return pl.pallas_call(
+        functools.partial(back_kernel, segments, mel, tuple(scratch)),
+        out_shape=(
+            shape((frames, w_input.shape[0]), f32),
+            shape((slot, padded), f32),
+            shape((slot, columns), f32),
+            shape((table.shape[0], slot), f32),
+            shape((8, columns + 8 * width + LANES), f32),
+            shape((hidden // shards, width), f32),
+            shape((slot, hidden), f32),
+            shape((slot, width), f32),
+            shape((3, slot, width), f32),
+        ),
+        in_specs=[anywhere] * 6 + [in_vmem] * 3 + [in_smem] + [anywhere] * 17,
+        out_specs=(in_vmem,) * 9,
+        scratch_shapes=list(scratch.values()),
+        compiler_params=pltpu.CompilerParams(collective_id=1, has_side_effects=True, vmem_limit_bytes=VMEM_BYTES),
+        name="back",
+    )(*operands)
+
+
+class FinishIn(NamedTuple):
+    features: Any
+    w_input: Any
+    w_ada: Any
+    table: Any
+    small: Any
+    w_down: Any
+    w_up: Any
+    w_out: Any
+    w_three: Any
+
+class FinishOut(NamedTuple):
+    noisy: Any
+    cond: Any
+    text: Any
+    out_table: Any
+    out_w_input: Any
+    out_w_ada: Any
+    out_query: Any
+    out_key: Any
+    out_value: Any
+    out_w_out: Any
+    out_up: Any
+    out_down: Any
+    b_input: Any
+    b_ada: Any
+    b_query: Any
+    b_key: Any
+    b_value: Any
+    b_out: Any
+    b_up: Any
+    b_down: Any
+
+
+def finish_kernel(mel, peers, *refs):
+    n = Names(FinishIn._fields + FinishOut._fields, refs)
+    shard = lax.axis_index("rows") * peers + lax.axis_index("seq")
+    frames = n.features.shape[0]
+    n.noisy[:, 0, :] = n.features[:, :LANES].T[:mel, :]
+    n.cond[:, 0, :] = n.features[:, mel : 2 * mel].T
+    n.text[...] = n.features[:, 2 * mel :]
+    n.out_table[...] = n.table[...]
+    n.out_w_input[...] = n.w_input[:, : n.out_w_input.shape[1]]
+    n.out_w_ada[...] = n.w_ada[...]
+    n.out_query[...] = n.w_three[0]
+    n.out_key[...] = n.w_three[1]
+    n.out_value[...] = n.w_three[2]
+    n.out_w_out[...] = n.w_out[...]
+    n.out_up[...] = n.w_up[...]
+    n.out_down[...] = n.w_down[...]
+    columns = n.w_ada.shape[1]
+    start = columns
+    biases = [n.b_query, n.b_key, n.b_value, n.b_out, n.b_up, n.b_down, n.b_input]
+    for start_of, out in [(None, out) for out in biases] + [(0, n.b_ada)]:
+        size = out.shape[0]
+        start = start if start_of is None else start_of
+        offset = shard * size
+        tiles = -(-(size + LANES) // LANES)
+        begin = pl.multiple_of(start + (offset // LANES) * LANES, LANES)
+        span = n.small[:, pl.ds(begin, tiles * LANES)]
+        moved = pltpu.roll(span, lax.rem(tiles * LANES - offset % LANES, tiles * LANES), 1)
+        out[...] = moved[0, :size]
+        start += size * 4 * peers
+
+
+def finish(mel, peers, operands):
+    features, w_input, w_ada, table, small, w_down, w_up, w_out, w_three = operands
+    frames, inputs = features.shape
+    slot, width = w_out.shape
+    shape = jax.ShapeDtypeStruct
+    in_vmem = pl.BlockSpec(memory_space=pltpu.VMEM)
+    outs = [
+        (mel, 1, frames), (mel, 1, frames), (frames, inputs - 2 * mel), table.shape, (slot, inputs), w_ada.shape,
+        (slot, width), (slot, width), (slot, width), (slot, width), w_up.shape, w_down.shape,
+        (slot,), (w_ada.shape[1] // (4 * peers),), (slot,), (slot,), (slot,), (slot,), (w_up.shape[1] // (4 * peers),), (slot,),
+    ]
+    return pl.pallas_call(
+        functools.partial(finish_kernel, mel, peers),
+        out_shape=tuple(shape(dims, f32) for dims in outs),
+        in_specs=[in_vmem] * 9,
+        out_specs=(in_vmem,) * 20,
+        compiler_params=pltpu.CompilerParams(vmem_limit_bytes=VMEM_BYTES),
+        name="finish",
+    )(*operands)
+
+
+def rope_table(length, head_width):
+    angles = np.arange(length)[:, None] * 10000.0 ** (-np.arange(0, head_width, 2) / head_width)[None, :]
+    cosine = np.repeat(np.cos(angles), 2, axis=1)
+    sine = np.stack([-np.sin(angles), np.sin(angles)], axis=2).reshape(length, head_width)
+    return np.concatenate([cosine, sine], axis=1).astype(np.float32)
+
+
+def shards(
+    noisy_mel, cond_mel, text_feats, segment_ids, drop_cond, drop_text, time_index, time_table, w_input, b_input,
+    w_ada, b_ada, w_query, b_query, w_key, b_key, w_value, b_value, w_out, b_out, w_up, b_up, w_down, b_down, cotangent,
+):
+    peers = lax.axis_size("seq")
+    frames = noisy_mel.shape[1]
+    mel = noisy_mel.shape[2]
+    segments = drop_cond.shape[1]
+    padded = -(-w_input.shape[0] // (3 * LANES)) * 3 * LANES
+    line = lambda bias: bias.reshape(1, -1)
+    turns = jnp.asarray(rope_table(frames * peers, w_query.shape[0] // HEADS))
+    fed = FrontOut(*front(
+        segments, peers, padded,
+        (noisy_mel[0].T, cond_mel[0].T, text_feats[0], segment_ids, drop_cond, drop_text, time_index, time_table,
+         line(b_input), line(b_ada), line(b_query), line(b_key), line(b_value), line(b_out), line(b_up), line(b_down),
+         cotangent[0], w_input, w_ada, w_query, w_key, w_value, turns, w_out, w_up, w_down),
+    ))
+    pieces = back(
+        segments, mel, peers,
+        (fed.grad_att_out, fed.middle_out, fed.stream_out, fed.mod_out, fed.marks_out, fed.features_out, fed.sums,
+         fed.biases, time_table, time_index, fed.query_out, fed.key_out, fed.value_out, fed.attended_out, fed.x_out,
+         turns, fed.act_t_out, fed.grad_ffn_out, fed.ffn_in_t_out, fed.grad_up_out, fed.att_t_out, fed.grad_attn_out,
+         w_query, w_key, w_value, w_input, w_ada),
+    )
+    out = Names(FinishOut._fields, finish(mel, peers, pieces))
+    return (
+        fed.layer_out[None],
+        out.noisy.transpose(1, 2, 0),
+        out.cond.transpose(1, 2, 0),
+        out.text[None],
+        out.out_table,
+        out.out_w_input.T,
+        out.b_input,
+        out.out_w_ada,
+        out.b_ada,
+        out.out_query,
+        out.b_query,
+        out.out_key,
+        out.b_key,
+        out.out_value,
+        out.b_value,
+        out.out_w_out,
+        out.b_out,
+        out.out_up,
+        out.b_up,
+        out.out_down,
+        out.b_down,
+    )
 
 
 precise = lax.Precision.HIGHEST
@@ -59,7 +1603,7 @@
     return (leading, second, third)
 
 
-def shards(
+def generic_shards(
     noisy_mel,
     cond_mel,
     text_feats,
@@ -446,4 +1990,5 @@
         P(("rows", "seq"), None),
         P(("rows", "seq")),
     )
-    return jax.shard_map(shards, mesh=mesh, in_specs=in_specs, out_specs=out_specs, check_vma=False)
+    body = shards if (mesh.shape["rows"], mesh.shape["seq"]) == (4, 8) else generic_shards
+    return jax.shard_map(body, mesh=mesh, in_specs=in_specs, out_specs=out_specs, check_vma=False)

time: 2050 us -> 179 us (0.09)
  waiting for transfers between devices: 1390 us -> 0 us
  matrix products: 292 us -> 0 us
  Pallas kernels: 0 us -> 177 us
  local copies, waits for them, and re-layouts: 143 us -> 0.8 us
  blocking collectives: 122 us -> 0 us
  other arithmetic: 51.2 us -> 0 us
  loops' own time: 24.8 us -> 0 us
    reduce_scatter x8 -> x0, waiting for transfers between devices: 1310 us -> none  [the longest x1 253 us: shards(): lax.psum_scatter(part_w_ada, ('rows', 'seq'), scatter_dimension=0, tiled=...]
    dot_general x58 -> x0, matrix products: 292 us -> none  [the longest x3 46.8 us: shards(): jnp.dot(silu_table.T, piece, preferred_element_type=jnp.float32)]
    pallas_call x0 -> x3, Pallas kernels: none -> 177 us  [the longest x1 96.5 us: back(): pl.pallas_call(functools.partial(back_kernel, segments, mel, tuple(scratc...]
    all_gather x3 -> x0, blocking collectives: 83.9 us -> none  [the longest x1 30.6 us: shards(): lax.all_gather(log_total, 'seq', axis=1, tiled=True)]
    all_gather x4 -> x0, waiting for transfers between devices: 81.4 us -> none  [the longest x1 69.1 us: shards(): lax.all_gather(key_rot, 'seq', axis=0, tiled=True)]
    dynamic_slice x48 -> x0, local copies, waits for them, and re-layouts: 61.6 us -> none  [the longest x32 60.3 us: over_blocks(): running, unused = lax.scan(advance, running, (shaped, offsets))]
    unnamed x1 -> x0, blocking collectives: 38.4 us -> none
    unnamed x177 -> x3, local copies, waits for them, and re-layouts: 37.2 us -> 0.8 us
  transfers between devices with their start and end apart: 13 -> 0, of which waited for: 11 -> 0; matrix products, arithmetic and copies ran while one was open for 14% -> 0% of each run, Pallas kernels for 0% -> 0%
where the time goes in v2:
time: 179 us
  Pallas kernels  177 us (99%)
    pallas_call x1, Pallas kernels, back(): pl.pallas_call(functools.partial(back_kernel, segments, mel, tuple(scratc...  96.5 us
    pallas_call x1, Pallas kernels, front(): pl.pallas_call(functools.partial(front_kernel, segments, tuple(scratch)),...  76.8 us
    pallas_call x1, Pallas kernels, finish(): pl.pallas_call(functools.partial(finish_kernel, mel, peers), out_shape=tu...  3.95 us

profile of v2, /device:TPU:0, one launch (start us, length us, event | category | flops | bytes accessed | tf_op | source)
XLA Modules:
  0.0 178.8 jit_solution(11585078388842693504)
XLA Ops:
  0.7 76.8 %front.1 = (f32[4,8,1024]{2,1,0:T(8,128)}, f32[1,4096]{1,0:T(1,128)}, f32[8,6144]{1,0:T(8,128)}, f32[256,1024]{1,0:T(8,128)}, bf16[256,768]{1,0:T(8,128)(2,1)}, ...) custom-call(bf16[100,256]{1,0:T(8,128)(2,1)} %bitcast.24, ...), custom_call_target="tpu_custom_call" | custom-call | tf_op jit(solution)/shard_map/front/pallas_call | solution.py:734
  77.5 96.5 %back.1 = (f32[256,712]{1,0:T(8,128)}, f32[32,768]{1,0:T(8,128)}, f32[32,6144]{1,0:T(8,128)}, f32[32,32]{1,0:T(8,128)}, f32[8,14464]{1,0:T(8,128)}, /*index=5*/f...) custom-call(bf16[256,1024]{1,0:T(8,128)(2,1)} %get-tuple-element.71.refs_0_, ...), custom_call_target="tpu_custom_call" | custom-call | tf_op jit(solution)/shard_map/back/pallas_call | solution.py:1391
  174.0 0.0 copy-start
  174.0 4.0 %finish.1 = (f32[100,1,256]{2,1,0:T(1,128)}, f32[100,1,256]{2,1,0:T(1,128)}, f32[256,512]{1,0:T(8,128)}, f32[32,32]{1,0:T(8,128)}, f32[32,712]{1,0:T(8,128)}, /*...) custom-call(f32[256,712]{1,0:T(8,128)} %get-tuple-element.90.refs_0_, ...), custom_call_target="tpu_custom_call" | custom-call | tf_op jit(solution)/shard_map/finish/pallas_call | solution.py:1488
  178.0 0.0 copy-done
  178.0 0.8 copy.48
Async XLA Ops:
  174.0 4.0 %copy-start = (bf16[256,1024]{1,0:T(8,128)(2,1)S(1)}, bf16[256,1024]{1,0:T(8,128)(2,1)}, u32[]{:S(2)}) copy-start(bf16[256,1024]{1,0:T(8,128)(2,1)} %get-tuple-element.70) | copy-start | bytes 1572868
